TPU v7x, 512 devices: a whole 4x8x8 slice. The times are simulated.
512 devices in a mesh: tile: 128 (over y, z_hi, x), mem: 4 (over z_lo, core).
Axes of the slice: x: 4, y: 8, z: 8 (z_hi: 4, z_lo: 2; z = z_hi * 2 + z_lo), core: 2. Of those that a mesh axis runs over, the one named last changes fastest.
Arguments:
- control_ens: float32 [32, 2, 32, 16384], P('mem', None, None, 'tile'), may hold values from -1.75 to 1.75
- control_static: float32 [2, 32, 16384], P(None, None, 'tile'), may hold values from -1.75 to 1.75
- static_sigma: float32 [2, 32, 16384], P(None, None, 'tile'), may hold values from 0.5 to 2
- east_coef: float32 [2, 32, 16384], P(None, None, 'tile'), may hold values from 0.04 to 0.22
- north_coef: float32 [2, 32, 16384], P(None, None, 'tile'), may hold values from 0.04 to 0.22
- perturbations: bfloat16 [32, 4, 2, 32, 16384], P('mem', None, None, None, 'tile'), may hold values from -6 to 6
- obs_counts: int32 [4, 128, 128], P('mem', 'tile'), may hold values from 0 to 4, as said below
- obs_rows: int32 [4, 128, 128, 4], P('mem', 'tile'), may hold values from 0 to 255
- footprints: bfloat16 [4, 128, 128, 4, 128], P('mem', 'tile'), may hold values from -1.5 to 1.5
- obs_values: float32 [4, 128, 128, 4], P('mem', 'tile'), may hold values from -6 to 6
- obs_precision: float32 [4, 128, 128, 4], P('mem', 'tile'), may hold values from 0.25 to 2
Outputs:
- grad_ensemble: float32 [32, 2, 32, 16384], P('mem', None, None, 'tile')
- grad_static: float32 [2, 32, 16384], P(None, None, 'tile')
Inputs may be any that keep to these rules, and one draw needn't show every extreme that they name: Slots c < obs_counts of a source and destination hold observations, the others are ignored; every source device fills all 4 slots to some destination.
All inputs are finite; a program needn't handle non-finite values.
Results may differ from a plain program's by a relative error of at most 0.0003.
Values may be sent and summed in bfloat16 or wider, within the bound.
No kernel may reach another device: no remote copies, remote signals or barrier semaphores. Data moves between devices by JAX's collectives and lax.ppermute only.
A program may use at most 64 MiB of HBM per device.

v0:
```python
import math

import jax
import jax.numpy as jnp
from jax import lax
from jax.sharding import PartitionSpec as P

SWEEPS = 2


def with_halo(cells, sides, width):
    for axis, dim in sides:
        count = lax.axis_size(axis)
        head = lax.slice_in_dim(cells, 0, width, axis=dim)
        tail = lax.slice_in_dim(cells, cells.shape[dim] - width, cells.shape[dim], axis=dim)
        cells = jnp.concatenate(
            [
                lax.ppermute(tail, axis, [(i, (i + 1) % count) for i in range(count)]),
                cells,
                lax.ppermute(head, axis, [((i + 1) % count, i) for i in range(count)]),
            ],
            axis=dim,
        )
    return cells


def shifted(x, axis, by):
    count = lax.axis_size(axis)
    return lax.ppermute(x, axis, [(i, (i + by) % count) for i in range(count)])


def diffuse(padded, coefficient):
    east_rate = coefficient[0]
    north_rate = coefficient[1][..., 1:-1]
    east_flux = east_rate[..., :-1] * (padded[..., 1:] - padded[..., :-1])
    center = padded[..., 1:-1]
    north_flux = north_rate[:, :-1, :] * (center[..., 1:, :] - center[..., :-1, :])
    zero_row = jnp.zeros_like(north_flux[..., :1, :])
    upper_flux = jnp.concatenate([north_flux, zero_row], axis=-2)
    lower_flux = jnp.concatenate([zero_row, north_flux], axis=-2)
    return center + (east_flux[..., 1:] - east_flux[..., :-1] + (upper_flux - lower_flux))


def smooth(grid_field, coefficient):
    for sweep_index in range(SWEEPS):
        padded = with_halo(grid_field, (("tile", 3),), 1)
        grid_field = diffuse(padded, coefficient)
    return grid_field


def on_device(
    control_ens,
    control_static,
    static_sigma,
    east_coef,
    north_coef,
    perturbations,
    obs_counts,
    obs_rows,
    footprints,
    obs_values,
    obs_precision,
):
    columns = control_static.shape[-1]
    west_edge = shifted(east_coef[..., -1:], "tile", 1)
    blank_edge = jnp.zeros_like(west_edge)
    coefficient = jnp.stack(
        [
            jnp.concatenate([west_edge, east_coef, blank_edge], axis=-1),
            jnp.concatenate([blank_edge, north_coef, blank_edge], axis=-1),
        ]
    )
    scale_ens = 1.0 / math.sqrt(control_ens.shape[0] * lax.axis_size("mem") - 1)
    stacked = jnp.concatenate([control_ens, control_static[None]], axis=0)
    smoothed = smooth(stacked, coefficient)
    partial_sum = jnp.sum(perturbations.astype(jnp.float32) * smoothed[:-1][:, None], axis=0)
    ens_sum = lax.psum(partial_sum, "mem")
    increment = scale_ens * ens_sum + static_sigma * smoothed[-1][None]
    rows_table = increment.reshape(-1, columns)
    table_rows = rows_table.shape[0]
    requested = obs_rows[0, 0]
    slot_index = jnp.arange(requested.shape[1], dtype=jnp.int32)
    live_slot = slot_index[None, :] < obs_counts[0, 0][:, None]
    precision_live = jnp.where(live_slot, obs_precision[0, 0], 0.0)
    incoming = lax.all_to_all(requested, "tile", split_axis=0, concat_axis=0, tiled=True)
    picked = jnp.take(rows_table, incoming, axis=0)
    returned = lax.all_to_all(picked, "tile", split_axis=0, concat_axis=0, tiled=True)
    weights_f = footprints[0, 0].astype(jnp.float32)
    model_obs = jnp.sum(weights_f * returned, axis=-1)
    residual = precision_live * (model_obs - obs_values[0, 0])
    weighted = lax.all_to_all(
        residual[..., None] * weights_f, "tile", split_axis=0, concat_axis=0, tiled=True
    )
    row_index = jnp.arange(table_rows, dtype=jnp.int32)
    selector = (row_index[:, None] == incoming.reshape(1, -1)).astype(jnp.float32)
    partial_grad = jnp.dot(
        selector,
        weighted.reshape(-1, columns),
        precision=lax.Precision.HIGHEST,
        preferred_element_type=jnp.float32,
    )
    gradient = lax.psum(partial_grad.reshape(increment.shape), "mem")
    ens_source = scale_ens * jnp.sum(perturbations.astype(jnp.float32) * gradient[None], axis=1)
    static_source = static_sigma * jnp.sum(gradient, axis=0)
    smoothed_back = smooth(jnp.concatenate([ens_source, static_source[None]], axis=0), coefficient)
    return (smoothed_back[:-1] + control_ens, smoothed_back[-1] + control_static)


def solution(mesh):
    placed = (
        P("mem", None, None, "tile"),
        P(None, None, "tile"),
        P(None, None, "tile"),
        P(None, None, "tile"),
        P(None, None, "tile"),
        P("mem", None, None, None, "tile"),
        P("mem", "tile", None),
        P("mem", "tile", None, None),
        P("mem", "tile", None, None, None),
        P("mem", "tile", None, None),
        P("mem", "tile", None, None),
    )
    return jax.shard_map(
        on_device,
        mesh=mesh,
        in_specs=placed,
        out_specs=(P("mem", None, None, "tile"), P(None, None, "tile")),
        check_vma=False,
    )
```

profile of v0, /device:TPU:1, one launch (start us, length us, event | category | flops | bytes accessed | tf_op | source)
XLA Modules:
  0.0 280.4 jit_solution(4614346782130585930)
XLA Ops:
  7.2 1.2 fusion.17
  8.4 16.7 %collective-permute-start.1 = (f32[9,2,32,1]{3,2,1,0:T(8,128)S(1)}, f32[9,2,32,1]{3,2,1,0:T(8,128)S(1)}, u32[]{:S(2)}, u32[]{:S(2)}) collective-permute-start(f32[9,2,32,1]{3,2,1,0:T(8,128)S(1)} %get-tuple-element.9), channel_id=1, source_target_pairs={{4,0},{8,4},{12,8},{16,12},{20,16},{24,20},{28,24},{32,28},{36,32}... | collective-permute-start | bytes 6920 | tf_op jit(solution)/shard_map/ppermute | solution.py:20
  25.2 1.9 collective-permute-start.2
  27.2 1.9 collective-permute-start
  29.9 13.6 %all-to-all-start = ((s32[128,1,4]{2,1,0:T(1,128)}), s32[128,1,4]{2,1,0:T(1,128)S(1)}, u32[]{:S(2)}, u32[]{:S(2)}) async-start(s32[128,1,4]{2,1,0:T(1,128)} %bitcast), calls=%async_computation | async-start | bytes 131072 | tf_op jit(solution)/shard_map/all_to_all | solution.py:85
  43.6 4.0 %collective-permute-done = f32[2,32,1]{2,1,0:T(8,128)S(1)} collective-permute-done((f32[2,32,1]{2,1,0:T(8,128)S(1)}, f32[2,32,1]{2,1,0:T(8,128)S(1)}, u32[]{:S(2)}, u32[]{:S(2)}) %collective-permute-start) | collective-permute-done | bytes 288 | tf_op jit(solution)/shard_map/ppermute | solution.py:29
  48.3 5.5 %collective-permute-start.3 = (f32[9,2,32,1]{3,2,1,0:T(8,128)S(1)}, f32[9,2,32,1]{3,2,1,0:T(8,128)S(1)}, u32[]{:S(2)}, u32[]{:S(2)}) collective-permute-start(f32[9,2,32,1]{3,2,1,0:T(8,128)S(1)} %get-tuple-element.7), channel_id=1, source_target_pairs={{4,0},{8,4},{12,8},{16,12},{20,16},{24,20},{28,24},{32,28},{36,32}... | collective-permute-start | bytes 6920 | tf_op jit(solution)/shard_map/ppermute | solution.py:20
  53.9 1.9 collective-permute-start.4
  56.7 1.9 collective-permute-done.3
  58.7 12.9 %collective-permute-done.4 = f32[9,2,32,1]{3,2,1,0:T(8,128)S(1)} collective-permute-done((f32[9,2,32,1]{3,2,1,0:T(8,128)S(1)}, f32[9,2,32,1]{3,2,1,0:T(8,128)S(1)}, u32[]{:S(2)}, u32[]{:S(2)}) %collective-permute-start.4) | collective-permute-done | bytes 2336 | tf_op jit(solution)/shard_map/ppermute | solution.py:18
  74.5 44.4 %all-reduce.11.cloned.1.call-done = f32[4,2,32,128]{3,2,1,0:T(8,128)} async-done(((f32[4,2,32,128]{3,2,1,0:T(8,128)}), f32[4,2,32,128]{3,2,1,0:T(8,128)}) %all-reduce.11.cloned.1.call-update) | async-done | bytes 131088 | tf_op jit(solution)/shard_map/psum | solution.py:77
  121.8 15.9 %all-to-all-start.1 = ((f32[128,4,128]{2,1,0:T(4,128)}), f32[128,4,128]{2,1,0:T(4,128)S(1)}, u32[]{:S(2)}, u32[]{:S(2)}) async-start(f32[128,4,128]{2,1,0:T(4,128)} %broadcast_select_fusion), calls=%async_computation.1 | async-start | bytes 524288 | tf_op jit(solution)/shard_map/all_to_all | solution.py:87
  138.0 16.1 %all-to-all-done.1 = f32[128,4,128]{2,1,0:T(4,128)S(1)} async-done(((f32[128,4,128]{2,1,0:T(4,128)}), f32[128,4,128]{2,1,0:T(4,128)S(1)}, u32[]{:S(2)}, u32[]{:S(2)}) %all-to-all-start.1) | async-done | bytes 262176 | tf_op jit(solution)/shard_map/all_to_all | solution.py:87
  156.0 6.2 %all-to-all-start.2 = ((f32[128,4,128]{2,1,0:T(4,128)}), f32[128,4,128]{2,1,0:T(4,128)S(1)}, u32[]{:S(2)}, u32[]{:S(2)}) async-start(f32[128,4,128]{2,1,0:T(4,128)} %convert_multiply_fusion.2), calls=%async_computation.2 | async-start | bytes 524288 | tf_op jit(solution)/shard_map/all_to_all | solution.py:91
  163.6 13.4 %all-to-all-done.2 = f32[128,4,128]{2,1,0:T(4,128)S(1)} async-done(((f32[128,4,128]{2,1,0:T(4,128)}), f32[128,4,128]{2,1,0:T(4,128)S(1)}, u32[]{:S(2)}, u32[]{:S(2)}) %all-to-all-start.2) | async-done | bytes 262176 | tf_op jit(solution)/shard_map/all_to_all | solution.py:91
  178.2 39.5 %all-reduce.13.cloned.1.call-done = f32[4,2,32,128]{3,2,1,0:T(8,128)} async-done(((f32[4,2,32,128]{3,2,1,0:T(8,128)}), f32[4,2,32,128]{3,2,1,0:T(8,128)}) %all-reduce.13.cloned.1.call-update) | async-done | bytes 131088 | tf_op jit(solution)/shard_map/psum | solution.py:102
  219.0 9.8 %collective-permute-start.5 = (f32[9,2,32,1]{3,2,1,0:T(8,128)S(1)}, f32[9,2,32,1]{3,2,1,0:T(8,128)S(1)}, u32[]{:S(2)}, u32[]{:S(2)}) collective-permute-start(f32[9,2,32,1]{3,2,1,0:T(8,128)S(1)} %get-tuple-element.5), channel_id=1, source_target_pairs={{4,0},{8,4},{12,8},{16,12},{20,16},{24,20},{28,24},{32,28},{36,32}... | collective-permute-start | bytes 6920 | tf_op jit(solution)/shard_map/ppermute | solution.py:20
  228.8 1.9 collective-permute-start.6
  230.8 6.7 %collective-permute-done.5 = f32[9,2,32,1]{3,2,1,0:T(8,128)S(1)} collective-permute-done((f32[9,2,32,1]{3,2,1,0:T(8,128)S(1)}, f32[9,2,32,1]{3,2,1,0:T(8,128)S(1)}, u32[]{:S(2)}, u32[]{:S(2)}) %collective-permute-start.5) | collective-permute-done | bytes 2336 | tf_op jit(solution)/shard_map/ppermute | solution.py:20
  237.5 13.1 %collective-permute-done.6 = f32[9,2,32,1]{3,2,1,0:T(8,128)S(1)} collective-permute-done((f32[9,2,32,1]{3,2,1,0:T(8,128)S(1)}, f32[9,2,32,1]{3,2,1,0:T(8,128)S(1)}, u32[]{:S(2)}, u32[]{:S(2)}) %collective-permute-start.6) | collective-permute-done | bytes 2336 | tf_op jit(solution)/shard_map/ppermute | solution.py:18
  251.1 1.9 collective-permute-start.7
  253.1 3.4 %collective-permute-start.8 = (f32[9,2,32,1]{3,2,1,0:T(8,128)S(1)}, f32[9,2,32,1]{3,2,1,0:T(8,128)S(1)}, u32[]{:S(2)}, u32[]{:S(2)}) collective-permute-start(f32[9,2,32,1]{3,2,1,0:T(8,128)S(1)} %get-tuple-element.2), channel_id=1, source_target_pairs={{0,4},{4,8},{8,12},{12,16},{16,20},{20,24},{24,28},{28,32},{32,36}... | collective-permute-start | bytes 6920 | tf_op jit(solution)/shard_map/ppermute | solution.py:18
  256.5 3.0 %collective-permute-done.7 = f32[9,2,32,1]{3,2,1,0:T(8,128)S(1)} collective-permute-done((f32[9,2,32,1]{3,2,1,0:T(8,128)S(1)}, f32[9,2,32,1]{3,2,1,0:T(8,128)S(1)}, u32[]{:S(2)}, u32[]{:S(2)}) %collective-permute-start.7) | collective-permute-done | bytes 2336 | tf_op jit(solution)/shard_map/ppermute | solution.py:20
  259.5 12.3 %collective-permute-done.8 = f32[9,2,32,1]{3,2,1,0:T(8,128)S(1)} collective-permute-done((f32[9,2,32,1]{3,2,1,0:T(8,128)S(1)}, f32[9,2,32,1]{3,2,1,0:T(8,128)S(1)}, u32[]{:S(2)}, u32[]{:S(2)}) %collective-permute-start.8) | collective-permute-done | bytes 2336 | tf_op jit(solution)/shard_map/ppermute | solution.py:18
  (75 shorter events, 16.5 us)
Async XLA Ops:
  7.2 19.9 %copy-start.7 = (f32[2,32,128]{2,1,0:T(8,128)S(1)}, f32[2,32,128]{2,1,0:T(8,128)}, u32[]{:S(2)}) copy-start(f32[2,32,128]{2,1,0:T(8,128)} %param.14) | copy-start | bytes 98308
  7.2 21.9 %copy-start.8 = (s32[1,1,128,4]{2,3,1,0:T(4,128)S(1)}, s32[1,1,128,4]{2,3,1,0:T(4,128)}, u32[]{:S(2)}) copy-start(s32[1,1,128,4]{2,3,1,0:T(4,128)} %param.18) | copy-start | bytes 6148
  7.2 36.3 %copy-start.2 = (f32[2,32,128]{2,1,0:T(8,128)S(1)}, f32[2,32,128]{2,1,0:T(8,128)}, u32[]{:S(2)}) copy-start(f32[2,32,128]{2,1,0:T(8,128)} %param.12) | copy-start | bytes 98308
  7.2 36.3 %copy-start.5 = (f32[2,32,128]{2,1,0:T(8,128)S(1)}, f32[2,32,128]{2,1,0:T(8,128)}, u32[]{:S(2)}) copy-start(f32[2,32,128]{2,1,0:T(8,128)} %param.15) | copy-start | bytes 98308
  8.4 35.1 %copy-start = (f32[8,2,32,128]{3,2,1,0:T(8,128)S(1)}, f32[8,2,32,128]{3,2,1,0:T(8,128)}, u32[]{:S(2)}) copy-start(f32[8,2,32,128]{3,2,1,0:T(8,128)} %param.11) | copy-start | bytes 786436
  8.4 39.3 %collective-permute-start.1 = (f32[9,2,32,1]{3,2,1,0:T(8,128)S(1)}, f32[9,2,32,1]{3,2,1,0:T(8,128)S(1)}, u32[]{:S(2)}, u32[]{:S(2)}) collective-permute-start(f32[9,2,32,1]{3,2,1,0:T(8,128)S(1)} %get-tuple-element.9), channel_id=1, source_target_pairs={{4,0},{8,4},{12,8},{16,12},{20,16},{24,20},{28,24},{32,28},{36,32}... | collective-permute-start | bytes 6920 | tf_op jit(solution)/shard_map/ppermute | solution.py:20
  25.2 22.6 %collective-permute-start.2 = (f32[9,2,32,1]{3,2,1,0:T(8,128)S(1)}, f32[9,2,32,1]{3,2,1,0:T(8,128)S(1)}, u32[]{:S(2)}, u32[]{:S(2)}) collective-permute-start(f32[9,2,32,1]{3,2,1,0:T(8,128)S(1)} %get-tuple-element.8), channel_id=1, source_target_pairs={{0,4},{4,8},{8,12},{12,16},{16,20},{20,24},{24,28},{28,32},{32,36}... | collective-permute-start | bytes 6920 | tf_op jit(solution)/shard_map/ppermute | solution.py:18
  27.2 20.5 %collective-permute-start = (f32[2,32,1]{2,1,0:T(8,128)S(1)}, f32[2,32,1]{2,1,0:T(8,128)S(1)}, u32[]{:S(2)}, u32[]{:S(2)}) collective-permute-start(f32[2,32,1]{2,1,0:T(8,128)S(1)} %slice.114), channel_id=1, source_target_pairs={{0,4},{4,8},{8,12},{12,16},{16,20},{20,24},{24,28},{28,32},{32,36}... | collective-permute-start | bytes 776 | tf_op jit(solution)/shard_map/ppermute | solution.py:29
  29.9 26.7 %all-to-all-start = ((s32[128,1,4]{2,1,0:T(1,128)}), s32[128,1,4]{2,1,0:T(1,128)S(1)}, u32[]{:S(2)}, u32[]{:S(2)}) async-start(s32[128,1,4]{2,1,0:T(1,128)} %bitcast), calls=%async_computation | async-start | bytes 131072 | tf_op jit(solution)/shard_map/all_to_all | solution.py:85
  43.5 75.5 %all-reduce.11.cloned.1.call-start = ((), (), s32[]{:S(2)}) async-start(), calls=%async_computation.3 | async-start | bytes 262144 | tf_op jit(solution)/shard_map/psum | solution.py:77
  48.3 10.3 %collective-permute-start.3 = (f32[9,2,32,1]{3,2,1,0:T(8,128)S(1)}, f32[9,2,32,1]{3,2,1,0:T(8,128)S(1)}, u32[]{:S(2)}, u32[]{:S(2)}) collective-permute-start(f32[9,2,32,1]{3,2,1,0:T(8,128)S(1)} %get-tuple-element.7), channel_id=1, source_target_pairs={{4,0},{8,4},{12,8},{16,12},{20,16},{24,20},{28,24},{32,28},{36,32}... | collective-permute-start | bytes 6920 | tf_op jit(solution)/shard_map/ppermute | solution.py:20
  53.9 17.7 %collective-permute-start.4 = (f32[9,2,32,1]{3,2,1,0:T(8,128)S(1)}, f32[9,2,32,1]{3,2,1,0:T(8,128)S(1)}, u32[]{:S(2)}, u32[]{:S(2)}) collective-permute-start(f32[9,2,32,1]{3,2,1,0:T(8,128)S(1)} %get-tuple-element.6), channel_id=1, source_target_pairs={{0,4},{4,8},{8,12},{12,16},{16,20},{20,24},{24,28},{28,32},{32,36}... | collective-permute-start | bytes 6920 | tf_op jit(solution)/shard_map/ppermute | solution.py:18
  72.0 1.0 copy-start.1
  121.8 15.9 %copy-start.9 = (f32[1,1,128,4]{2,3,1,0:T(4,128)S(1)}, f32[1,1,128,4]{2,3,1,0:T(4,128)}, u32[]{:S(2)}) copy-start(f32[1,1,128,4]{2,3,1,0:T(4,128)} %param.20) | copy-start | bytes 6148
  121.8 16.0 %copy-start.10 = (f32[1,1,128,4]{2,3,1,0:T(4,128)S(1)}, f32[1,1,128,4]{2,3,1,0:T(4,128)}, u32[]{:S(2)}) copy-start(f32[1,1,128,4]{2,3,1,0:T(4,128)} %param.21) | copy-start | bytes 6148
  121.8 32.3 %all-to-all-start.1 = ((f32[128,4,128]{2,1,0:T(4,128)}), f32[128,4,128]{2,1,0:T(4,128)S(1)}, u32[]{:S(2)}, u32[]{:S(2)}) async-start(f32[128,4,128]{2,1,0:T(4,128)} %broadcast_select_fusion), calls=%async_computation.1 | async-start | bytes 524288 | tf_op jit(solution)/shard_map/all_to_all | solution.py:87
  137.7 16.4 %copy-start.3 = (bf16[1,1,128,4,128]{4,3,2,1,0:T(4,128)(2,1)S(1)}, bf16[1,1,128,4,128]{4,3,2,1,0:T(4,128)(2,1)}, u32[]{:S(2)}) copy-start(bf16[1,1,128,4,128]{4,3,2,1,0:T(4,128)(2,1)} %param.19) | copy-start | bytes 393220
  156.0 21.1 %all-to-all-start.2 = ((f32[128,4,128]{2,1,0:T(4,128)}), f32[128,4,128]{2,1,0:T(4,128)S(1)}, u32[]{:S(2)}, u32[]{:S(2)}) async-start(f32[128,4,128]{2,1,0:T(4,128)} %convert_multiply_fusion.2), calls=%async_computation.2 | async-start | bytes 524288 | tf_op jit(solution)/shard_map/all_to_all | solution.py:91
  162.1 55.6 %all-reduce.13.cloned.1.call-start = ((), (), s32[]{:S(2)}) async-start(), calls=%async_computation.4 | async-start | bytes 262144 | tf_op jit(solution)/shard_map/psum | solution.py:102
  217.7 1.0 copy-start.4
  219.0 18.5 %collective-permute-start.5 = (f32[9,2,32,1]{3,2,1,0:T(8,128)S(1)}, f32[9,2,32,1]{3,2,1,0:T(8,128)S(1)}, u32[]{:S(2)}, u32[]{:S(2)}) collective-permute-start(f32[9,2,32,1]{3,2,1,0:T(8,128)S(1)} %get-tuple-element.5), channel_id=1, source_target_pairs={{4,0},{8,4},{12,8},{16,12},{20,16},{24,20},{28,24},{32,28},{36,32}... | collective-permute-start | bytes 6920 | tf_op jit(solution)/shard_map/ppermute | solution.py:20
  228.8 21.8 %collective-permute-start.6 = (f32[9,2,32,1]{3,2,1,0:T(8,128)S(1)}, f32[9,2,32,1]{3,2,1,0:T(8,128)S(1)}, u32[]{:S(2)}, u32[]{:S(2)}) collective-permute-start(f32[9,2,32,1]{3,2,1,0:T(8,128)S(1)} %get-tuple-element.4), channel_id=1, source_target_pairs={{0,4},{4,8},{8,12},{12,16},{16,20},{20,24},{24,28},{28,32},{32,36}... | collective-permute-start | bytes 6920 | tf_op jit(solution)/shard_map/ppermute | solution.py:18
  251.1 8.4 %collective-permute-start.7 = (f32[9,2,32,1]{3,2,1,0:T(8,128)S(1)}, f32[9,2,32,1]{3,2,1,0:T(8,128)S(1)}, u32[]{:S(2)}, u32[]{:S(2)}) collective-permute-start(f32[9,2,32,1]{3,2,1,0:T(8,128)S(1)} %get-tuple-element.3), channel_id=1, source_target_pairs={{4,0},{8,4},{12,8},{16,12},{20,16},{24,20},{28,24},{32,28},{36,32}... | collective-permute-start | bytes 6920 | tf_op jit(solution)/shard_map/ppermute | solution.py:20
  253.1 18.8 %collective-permute-start.8 = (f32[9,2,32,1]{3,2,1,0:T(8,128)S(1)}, f32[9,2,32,1]{3,2,1,0:T(8,128)S(1)}, u32[]{:S(2)}, u32[]{:S(2)}) collective-permute-start(f32[9,2,32,1]{3,2,1,0:T(8,128)S(1)} %get-tuple-element.2), channel_id=1, source_target_pairs={{0,4},{4,8},{8,12},{12,16},{16,20},{20,24},{24,28},{28,32},{32,36}... | collective-permute-start | bytes 6920 | tf_op jit(solution)/shard_map/ppermute | solution.py:18
  (2 other events, 1.4 us)
Sparse Core Ops, SparseCore 0:
  73.9 44.9 all-reduce.10
  178.3 39.3 all-reduce.12
where the time goes:
time: 281 us; the launch traced here: 280 us
  waiting for transfers between devices  168 us (60%)
  starting transfers between devices  80.7 us (29%)
  between operations  14.5 us (5%)
  other arithmetic  10.3 us (4%)
  local copies, waits for them, and re-layouts  5.54 us (2%)
    psum x1, waiting for transfers between devices, on_device(): ens_sum = lax.psum(partial_sum, 'mem')  44.4 us
    psum x1, waiting for transfers between devices, on_device(): gradient = lax.psum(partial_grad.reshape(increment.shape), 'mem')  39.5 us
    ppermute x4, waiting for transfers between devices, with_halo(): lax.ppermute(tail, axis, [(i, (i + 1) % count) for i in range(count)])  38.3 us
    ppermute x4, starting transfers between devices, with_halo(): lax.ppermute(head, axis, [((i + 1) % count, i) for i in range(count)])  34 us
    all_to_all x1, waiting for transfers between devices, on_device(): lax.all_to_all(picked, 'tile', split_axis=0, concat_axis=0, tiled=True)  16.1 us
    all_to_all x1, starting transfers between devices, on_device(): lax.all_to_all(picked, 'tile', split_axis=0, concat_axis=0, tiled=True)  15.9 us
    all_to_all x1, starting transfers between devices, on_device(): lax.all_to_all(requested, 'tile', split_axis=0, concat_axis=0, tiled=True)  13.6 us
    all_to_all x1, waiting for transfers between devices, on_device(): lax.all_to_all(residual[..., None] * weights_f, 'tile', split_axis=0, con...  13.4 us
  transfers between devices with their start and end apart: 14, of which 12 were waited for; matrix products, arithmetic and copies ran while one was open for 1% of the time, Pallas kernels for 0%

commit v1 on v0

v1 whole, which is shorter than its diff:
```python
import math

import jax
import jax.numpy as jnp
from jax import lax
from jax.experimental import pallas as pl
from jax.experimental.pallas import tpu as pltpu
from jax.sharding import PartitionSpec as P

SWEEPS = 2
F32 = jnp.float32
BF16 = jnp.bfloat16
VMEM = pl.BlockSpec(memory_space=pltpu.VMEM)


def call(body, out, flops, traffic, *operands):
    return pl.pallas_call(
        body,
        out_shape=out,
        in_specs=[VMEM] * len(operands),
        out_specs=jax.tree.map(lambda _: VMEM, out),
        cost_estimate=pl.CostEstimate(flops=int(flops), bytes_accessed=int(traffic), transcendentals=0),
        compiler_params=pltpu.CompilerParams(vmem_limit_bytes=32 * 1024 * 1024),
    )(*operands)


def shape(dims, kind=F32):
    return jax.ShapeDtypeStruct(dims, kind)


def shifted(x, axis, by):
    count = lax.axis_size(axis)
    return lax.ppermute(x, axis, [(i, (i + by) % count) for i in range(count)])


def everyone(copies):
    return lax.all_to_all(copies, "mem", split_axis=0, concat_axis=0, tiled=True)


def split_two(x):
    high = x.astype(BF16)
    return high, (x - high.astype(F32)).astype(BF16)


def split_three(x):
    high = x.astype(BF16)
    rest = x - high.astype(F32)
    mid = rest.astype(BF16)
    return high, mid, (rest - mid.astype(F32)).astype(BF16)


def pack_edges(fields, east_ref, west_ref):
    rows, columns = fields[0].shape
    lane = lax.broadcasted_iota(jnp.int32, (rows, columns), 1)
    east = jnp.zeros((rows, columns), F32)
    west = jnp.zeros((rows, columns), F32)
    for f, u in enumerate(fields):
        here = (lane == 2 * f) | (lane == 2 * f + 1)
        east = jnp.where(here, pltpu.roll(u, (2 * f + 2) % columns, 1), east)
        west = jnp.where(here, pltpu.roll(u, 2 * f, 1) if f else u, west)
    east_ref[...] = east
    west_ref[...] = west


def unpack_edges(from_west, from_east, f, lane):
    columns = from_west.shape[1]
    left = pltpu.roll(from_west, columns - 2 - 2 * f, 1)
    right = pltpu.roll(from_east, (columns - 2 * f) % columns, 1) if f else from_east
    return jnp.where(lane >= columns - 2, left, jnp.where(lane < 2, right, 0.0))


def diffuse(u, h, e, eh, n, nh, lane):
    rows, columns = u.shape

    def pair_roll(a, b, by, edge):
        ra, rb = pltpu.roll(a, by, 1), pltpu.roll(b, by, 1)
        at = lane == edge
        return jnp.where(at, rb, ra), jnp.where(at, ra, rb)

    ue, he = pair_roll(u, h, columns - 1, columns - 1)
    flux, flux_h = e * (ue - u), eh * (he - h)
    west, west_h = pair_roll(flux, flux_h, 1, 0)

    def vertical(a, c):
        up = c * (pltpu.roll(a, rows - 1, 0) - a)
        return up - pltpu.roll(up, 1, 0)

    return (
        u + ((flux - west) + vertical(u, n)),
        h + ((flux_h - west_h) + vertical(h, nh)),
    )


def coefficients(e_ref, n_ref, from_west, from_east, fields, lane, latitudes):
    e, n = e_ref[...], n_ref[...]
    eh = unpack_edges(from_west, from_east, fields, lane)
    nh = unpack_edges(from_west, from_east, fields + 1, lane)
    row = lax.broadcasted_iota(jnp.int32, e.shape, 0)
    last = (row & (latitudes - 1)) == latitudes - 1
    return e, eh, jnp.where(last, 0.0, n), jnp.where(last, 0.0, nh)


def edges_body(ens_ref, static_ref, e_ref, n_ref, east_ref, west_ref):
    fields = [ens_ref[m] for m in range(ens_ref.shape[0])]
    pack_edges(fields + [static_ref[...], e_ref[...], n_ref[...]], east_ref, west_ref)


def message_body(fp_ref, counts_ref, rows_ref, values_ref, precision_ref, out_ref):
    cap, dests = rows_ref.shape
    slot = lax.broadcasted_iota(jnp.int32, (cap, dests), 0)
    live = slot < counts_ref[...]
    items = [rows_ref[...].astype(F32)]
    items += [x.astype(F32) for x in split_three(values_ref[...])]
    items += [x.astype(F32) for x in split_three(jnp.where(live, precision_ref[...], 0.0))]
    items += [jnp.zeros((cap, dests), F32)]
    stacked = [x[c : c + 1] for c in range(cap) for x in items]
    stacked.append(jnp.zeros((out_ref.shape[2] - len(stacked), dests), F32))
    meta = jnp.concatenate(stacked, axis=0).T
    place = lax.broadcasted_iota(jnp.int32, out_ref.shape, 1)
    out_ref[...] = jnp.where(
        place == cap, meta[:, None, :], fp_ref[...].astype(F32)
    ).astype(BF16)


def increment_body(latitudes, scale, share, ens_ref, static_ref, sigma_ref, e_ref, n_ref, pert_ref, west_ref, east_ref, out_ref):
    members, slots = pert_ref.shape[:2]
    rows = e_ref.shape[0]
    lane = lax.broadcasted_iota(jnp.int32, e_ref.shape, 1)
    from_west, from_east = west_ref[...], east_ref[...]
    coef = coefficients(e_ref, n_ref, from_west, from_east, members + 1, lane, latitudes)

    def smooth(u, f):
        h = unpack_edges(from_west, from_east, f, lane)
        for _ in range(SWEEPS):
            u, h = diffuse(u, h, *coef, lane)
        return u

    total = [jnp.zeros(e_ref.shape, F32) for _ in range(slots)]
    for m in range(members):
        u = smooth(ens_ref[m], m)
        for t in range(slots):
            total[t] = total[t] + pert_ref[m, t].astype(F32) * u
    static = (share * sigma_ref[...]) * smooth(static_ref[...], members)
    for t in range(slots):
        part = scale * total[t] + static
        for g in range(out_ref.shape[0]):
            out_ref[g, t * rows : (t + 1) * rows, :] = part


def observe_body(cap, parts_ref, seen_ref, out_ref):
    table = parts_ref[0]
    for g in range(1, parts_ref.shape[0]):
        table = table + parts_ref[g]
    rows, columns = table.shape
    high, low = split_two(table)
    seen = seen_ref[...]
    count = seen.shape[0]
    room = seen.shape[0] // seen_ref.shape[0]
    group = 8
    eye_shape = (group * cap, columns)
    eye = (
        lax.broadcasted_iota(jnp.int32, eye_shape, 0) == lax.broadcasted_iota(jnp.int32, eye_shape, 1)
    ).astype(F32).astype(BF16)
    contract = (((1,), (1,)), ((), ()))
    got = lax.dot_general(high, seen, contract, preferred_element_type=F32)
    got = got + lax.dot_general(low, seen, contract, preferred_element_type=F32)
    meta = lax.dot_general(eye, seen, contract, preferred_element_type=F32)
    place = lax.broadcasted_iota(jnp.int32, (group, count), 1) & (group - 1)
    facts = jnp.zeros((group, count), F32)
    for c in range(cap):
        part = pltpu.roll(meta[c * group : (c + 1) * group], count - (cap - c), 1)
        facts = jnp.where(place == c, part, facts)
    row_of = jnp.where(place[:1] < cap, facts[0:1], -1.0).astype(jnp.int32)
    value = (facts[1:2] + facts[2:3]) + facts[3:4]
    precision = (facts[4:5] + facts[5:6]) + facts[6:7]
    hit = lax.broadcasted_iota(jnp.int32, (rows, count), 0) == row_of
    model = jnp.sum(jnp.where(hit, got, 0.0), axis=0, keepdims=True)
    residual = precision * (model - value)
    out = None
    for piece in split_two(residual):
        spread = jnp.where(hit, piece.astype(F32), 0.0).astype(BF16)
        term = jnp.dot(spread, seen, preferred_element_type=F32)
        out = term if out is None else out + term
    for g in range(out_ref.shape[0]):
        out_ref[g] = out


def source_body(scale, parts_ref, pert_ref, sigma_ref, out_ref, east_ref, west_ref):
    members, slots, rows = pert_ref.shape[:3]
    gradient = []
    for t in range(slots):
        span = slice(t * rows, (t + 1) * rows)
        g = parts_ref[0, span, :]
        for k in range(1, parts_ref.shape[0]):
            g = g + parts_ref[k, span, :]
        gradient.append(g)
    fields = []
    for m in range(members):
        u = pert_ref[m, 0].astype(F32) * gradient[0]
        for t in range(1, slots):
            u = u + pert_ref[m, t].astype(F32) * gradient[t]
        u = scale * u
        out_ref[m] = u
        fields.append(u)
    u = gradient[0]
    for t in range(1, slots):
        u = u + gradient[t]
    u = sigma_ref[...] * u
    out_ref[members] = u
    pack_edges(fields + [u], east_ref, west_ref)


def result_body(latitudes, source_ref, ens_ref, static_ref, e_ref, n_ref, west0_ref, east0_ref, west_ref, east_ref, ens_out, static_out):
    members = ens_ref.shape[0]
    lane = lax.broadcasted_iota(jnp.int32, e_ref.shape, 1)
    coef = coefficients(e_ref, n_ref, west0_ref[...], east0_ref[...], members + 1, lane, latitudes)
    from_west, from_east = west_ref[...], east_ref[...]
    for f in range(members + 1):
        u = source_ref[f]
        h = unpack_edges(from_west, from_east, f, lane)
        for _ in range(SWEEPS):
            u, h = diffuse(u, h, *coef, lane)
        if f < members:
            ens_out[f] = u + ens_ref[f]
        else:
            static_out[...] = u + static_ref[...]


def on_device(
    control_ens,
    control_static,
    static_sigma,
    east_coef,
    north_coef,
    perturbations,
    obs_counts,
    obs_rows,
    footprints,
    obs_values,
    obs_precision,
):
    members, levels, latitudes, columns = control_ens.shape
    slots = perturbations.shape[1]
    rows = levels * latitudes
    table_rows = slots * rows
    groups = lax.axis_size("mem")
    scale = 1.0 / math.sqrt(members * groups - 1)
    ens = control_ens.reshape(members, rows, columns)
    static = control_static.reshape(rows, columns)
    sigma = static_sigma.reshape(rows, columns)
    e = east_coef.reshape(rows, columns)
    n = north_coef.reshape(rows, columns)
    pert = perturbations.reshape(members, slots, rows, columns)
    tiles, cap = obs_rows.shape[2:]

    field = shape((rows, columns))
    to_east, to_west = call(edges_body, (field, field), 1e6, 2e6, ens, static, e, n)
    west0 = shifted(to_east, "tile", 1)
    east0 = shifted(to_west, "tile", -1)

    room = 8
    padded = jnp.pad(footprints[0, 0], ((0, 0), (0, room - cap), (0, 0)))
    message = call(
        message_body,
        shape((tiles, room, columns), BF16),
        1e6,
        1e6,
        padded,
        obs_counts[0],
        obs_rows[0, 0].T,
        obs_values[0, 0].T,
        obs_precision[0, 0].T,
    )
    seen = lax.all_to_all(message, "tile", split_axis=0, concat_axis=0, tiled=True)

    partial = call(
        lambda *refs: increment_body(latitudes, scale, 1.0 / groups, *refs),
        shape((groups, table_rows, columns)),
        1e7,
        4e6,
        ens,
        static,
        sigma,
        e,
        n,
        pert,
        west0,
        east0,
    )
    parts = everyone(partial)
    partial_grad = call(
        lambda *refs: observe_body(cap, *refs),
        shape((groups, table_rows, columns)),
        3e8,
        4e6,
        parts,
        seen.reshape(tiles * room, columns),
    )
    grad_parts = everyone(partial_grad)
    source, to_east, to_west = call(
        lambda *refs: source_body(scale, *refs),
        (shape((members + 1, rows, columns)), field, field),
        1e7,
        2e6,
        grad_parts,
        pert,
        sigma,
    )
    west1 = shifted(to_east, "tile", 1)
    east1 = shifted(to_west, "tile", -1)
    ens_out, static_out = call(
        lambda *refs: result_body(latitudes, *refs),
        (shape(ens.shape), field),
        1e7,
        2e6,
        source,
        ens,
        static,
        e,
        n,
        west0,
        east0,
        west1,
        east1,
    )
    return ens_out.reshape(control_ens.shape), static_out.reshape(control_static.shape)


def solution(mesh):
    placed = (
        P("mem", None, None, "tile"),
        P(None, None, "tile"),
        P(None, None, "tile"),
        P(None, None, "tile"),
        P(None, None, "tile"),
        P("mem", None, None, None, "tile"),
        P("mem", "tile", None),
        P("mem", "tile", None, None),
        P("mem", "tile", None, None, None),
        P("mem", "tile", None, None),
        P("mem", "tile", None, None),
    )
    return jax.shard_map(
        on_device,
        mesh=mesh,
        in_specs=placed,
        out_specs=(P("mem", None, None, "tile"), P(None, None, "tile")),
        check_vma=False,
    )
```

time: 281 us -> 81.6 us (0.29)
  waiting for transfers between devices: 168 us -> 2.53 us
  starting transfers between devices: 80.7 us -> 44.2 us
  blocking collectives: 0 us -> 24.4 us
  between operations: 14.5 us -> 0.8 us
  other arithmetic: 10.3 us -> 0 us
  Pallas kernels: 0 us -> 7.65 us
  local copies, waits for them, and re-layouts: 5.54 us -> 1.66 us
    psum x2 -> x0, waiting for transfers between devices: 83.9 us -> none  [the longest x1 44.4 us: on_device(): ens_sum = lax.psum(partial_sum, 'mem')]
    ppermute x8 -> x0, waiting for transfers between devices: 50 us -> none  [the longest x4 38.3 us: with_halo(): lax.ppermute(tail, axis, [(i, (i + 1) % count) for i in range(count)])]
    ppermute x8 -> x0, starting transfers between devices: 43.1 us -> none  [the longest x4 34 us: with_halo(): lax.ppermute(head, axis, [((i + 1) % count, i) for i in range(count)])]
    all_to_all x3 -> x1, waiting for transfers between devices: 30.3 us -> 0.53 us  [on_device(): lax.all_to_all(message, 'tile', split_axis=0, concat_axis=0, tiled=True)]
    all_to_all x0 -> x2, blocking collectives: none -> 24.4 us  [everyone(): lax.all_to_all(copies, 'mem', split_axis=0, concat_axis=0, tiled=True)]
    ppermute x1 -> x4, starting transfers between devices: 1.91 us -> 23.2 us  [shifted(): return lax.ppermute(x, axis, [(i, (i + by) % count) for i in range(count)])]
    all_to_all x3 -> x1, starting transfers between devices: 35.7 us -> 20.9 us  [on_device(): lax.all_to_all(message, 'tile', split_axis=0, concat_axis=0, tiled=True)]
    pallas_call x0 -> x6, Pallas kernels: none -> 7.65 us  [call(): pl.pallas_call(body, out_shape=out, in_specs=[VMEM] * len(operands), out_...]
  transfers between devices with their start and end apart: 14 -> 5, of which waited for: 12 -> 3; matrix products, arithmetic and copies ran while one was open for 1% -> 0% of each run, Pallas kernels for 0% -> 3%
where the time goes in v1:
time: 81.6 us; the launch traced here: 81.2 us
  starting transfers between devices  44.2 us (54%)
  blocking collectives  24.4 us (30%)
  Pallas kernels  7.65 us (9%)
  waiting for transfers between devices  2.53 us (3%)
  local copies, waits for them, and re-layouts  1.66 us (2%)
    all_to_all x2, blocking collectives, everyone(): lax.all_to_all(copies, 'mem', split_axis=0, concat_axis=0, tiled=True)  24.4 us
    ppermute x4, starting transfers between devices, shifted(): return lax.ppermute(x, axis, [(i, (i + by) % count) for i in range(count)])  23.2 us
    all_to_all x1, starting transfers between devices, on_device(): lax.all_to_all(message, 'tile', split_axis=0, concat_axis=0, tiled=True)  20.9 us
    pallas_call x6, Pallas kernels, call(): pl.pallas_call(body, out_shape=out, in_specs=[VMEM] * len(operands), out_...  7.65 us
    ppermute x4, waiting for transfers between devices, shifted(): return lax.ppermute(x, axis, [(i, (i + by) % count) for i in range(count)])  2 us
  transfers between devices with their start and end apart: 5, of which 3 were waited for; matrix products, arithmetic and copies ran while one was open for 0% of the time, Pallas kernels for 3%

profile of v1, /device:TPU:1, one launch (start us, length us, event | category | flops | bytes accessed | tf_op | source)
XLA Modules:
  0.0 81.2 jit_solution(56031534861818018)
XLA Ops:
  0.6 1.0 %pad.4.fp_ref = bf16[128,8,128]{2,1,0:T(8,128)(2,1)S(1)} pad(bf16[128,4,128]{2,1,0:T(4,128)(2,1)} %bitcast.41, bf16[]{:T(256)} %constant.2.clone.1), padding=0_0x0_4x0_0 | pad | bytes 393218 | tf_op jit(solution)/shard_map/jit(_pad)/pad | solution.py:262
  1.6 0.0 copy-start.7
  1.6 0.0 copy-start.6
  1.6 0.0 copy-start.9
  1.7 0.6 copy-done.7
  2.3 0.0 copy-done.6
  2.3 0.9 %shard_map.124 = bf16[128,8,128]{2,1,0:T(8,128)(2,1)} custom-call(bf16[128,8,128]{2,1,0:T(8,128)(2,1)S(1)} %pad.4.fp_ref, s32[1,128]{1,0:T(1,128)S(1)} %bitcast.40, s32[4,128]{1,0:T(4,128)S(1)} %bitcast.37, f32[4,128]{1,0:T(4,128)S(1)} %bitcast.38, f32[4,128]{1,0:T(4,128)S(1)} %bitcast.39), custom_call_target="tpu_custom_call" | custom-call | flops 1000000 | bytes 1000000 | tf_op jit(solution)/shard_map/pallas_call | solution.py:17
  3.2 20.9 %all-to-all-start.1 = ((bf16[128,8,128]{2,1,0:T(8,128)(2,1)}), bf16[128,8,128]{2,1,0:T(8,128)(2,1)S(1)}, u32[]{:S(2)}, u32[]{:S(2)}) async-start(bf16[128,8,128]{2,1,0:T(8,128)(2,1)} %shard_map.124), calls=%async_computation.1 | async-start | bytes 524288 | tf_op jit(solution)/shard_map/all_to_all | solution.py:274
  24.2 0.0 copy-start.5
  24.2 0.2 shard_map.122
  24.4 2.5 %collective-permute-start = (f32[64,128]{1,0:T(8,128)S(1)}, f32[64,128]{1,0:T(8,128)S(1)}, u32[]{:S(2)}, u32[]{:S(2)}) collective-permute-start(f32[64,128]{1,0:T(8,128)S(1)} %get-tuple-element.9), channel_id=1, source_target_pairs={{0,4},{4,8},{8,12},{12,16},{16,20},{20,24},{24,28},{28,32},{32,36}... | collective-permute-start | bytes 98312 | tf_op jit(solution)/shard_map/ppermute | solution.py:33
  26.9 9.1 %collective-permute-start.1 = (f32[64,128]{1,0:T(8,128)S(1)}, f32[64,128]{1,0:T(8,128)S(1)}, u32[]{:S(2)}, u32[]{:S(2)}) collective-permute-start(f32[64,128]{1,0:T(8,128)S(1)} %get-tuple-element.10), channel_id=1, source_target_pairs={{0,508},{4,0},{8,4},{12,8},{16,12},{20,16},{24,20},{28,24},{32,28}... | collective-permute-start | bytes 98312 | tf_op jit(solution)/shard_map/ppermute | solution.py:33
  36.1 1.0 %collective-permute-done.refs_6_.refs_5_ = f32[64,128]{1,0:T(8,128)S(1)} collective-permute-done((f32[64,128]{1,0:T(8,128)S(1)}, f32[64,128]{1,0:T(8,128)S(1)}, u32[]{:S(2)}, u32[]{:S(2)}) %collective-permute-start) | collective-permute-done | bytes 32800 | tf_op jit(solution)/shard_map/ppermute | solution.py:33
  37.0 0.0 collective-permute-done.1.refs_7_.refs_6_
  37.1 2.3 %shard_map.123 = f32[4,256,128]{2,1,0:T(8,128)S(1)} custom-call(f32[8,64,128]{2,1,0:T(8,128)S(1)} %bitcast.21, f32[64,128]{1,0:T(8,128)S(1)} %bitcast.27, f32[64,128]{1,0:T(8,128)S(1)} %bitcast.35, f32[64,128]{1,0:T(8,128)S(1)} %bitcast.30, f32[64,128]{1,0:T(8,128)S(1)} %bitcast.33, bf16[8,4,64,128]{3,2,1,0:T(8,128)(2,1)S(1)} %bitcast.23, ...), custom_call_target="tpu_custom_call" | custom-call | flops 10000000 | bytes 4000000 | tf_op jit(solution)/shard_map/pallas_call | solution.py:17
  39.3 0.5 all-to-all-done.1
  39.9 13.1 %all_to_all.15.refs_0_ = f32[4,256,128]{2,1,0:T(8,128)S(1)} all-to-all(f32[4,256,128]{2,1,0:T(8,128)S(1)} %shard_map.123), channel_id=1, replica_groups=mesh['tile'=128,'mem'=4] {'mem'}, dimensions={0} | all-to-all | bytes 1048576 | tf_op jit(solution)/shard_map/all_to_all | solution.py:37
  53.0 1.2 %shard_map.125 = f32[4,256,128]{2,1,0:T(8,128)S(1)} custom-call(f32[4,256,128]{2,1,0:T(8,128)S(1)} %all_to_all.15.refs_0_, bf16[1024,128]{1,0:T(8,128)(2,1)S(1)} %bitcast.25), custom_call_target="tpu_custom_call" | custom-call | flops 300000000 | bytes 4000000 | tf_op jit(solution)/shard_map/pallas_call | solution.py:17
  54.2 11.2 %all_to_all.16.refs_0_ = f32[4,256,128]{2,1,0:T(8,128)S(1)} all-to-all(f32[4,256,128]{2,1,0:T(8,128)S(1)} %shard_map.125), channel_id=1, replica_groups=mesh['tile'=128,'mem'=4] {'mem'}, dimensions={0} | all-to-all | bytes 1048576 | tf_op jit(solution)/shard_map/all_to_all | solution.py:37
  65.4 0.2 shard_map.126
  65.7 2.2 %collective-permute-start.2 = (f32[64,128]{1,0:T(8,128)S(1)}, f32[64,128]{1,0:T(8,128)S(1)}, u32[]{:S(2)}, u32[]{:S(2)}) collective-permute-start(f32[64,128]{1,0:T(8,128)S(1)} %get-tuple-element.12), channel_id=1, source_target_pairs={{0,4},{4,8},{8,12},{12,16},{16,20},{20,24},{24,28},{28,32},{32,36}... | collective-permute-start | bytes 98312 | tf_op jit(solution)/shard_map/ppermute | solution.py:33
  67.8 9.4 %collective-permute-start.3 = (f32[64,128]{1,0:T(8,128)S(1)}, f32[64,128]{1,0:T(8,128)S(1)}, u32[]{:S(2)}, u32[]{:S(2)}) collective-permute-start(f32[64,128]{1,0:T(8,128)S(1)} %get-tuple-element.13), channel_id=1, source_target_pairs={{0,508},{4,0},{8,4},{12,8},{16,12},{20,16},{24,20},{28,24},{32,28}... | collective-permute-start | bytes 98312 | tf_op jit(solution)/shard_map/ppermute | solution.py:33
  77.3 1.0 %collective-permute-done.3.refs_8_ = f32[64,128]{1,0:T(8,128)S(1)} collective-permute-done((f32[64,128]{1,0:T(8,128)S(1)}, f32[64,128]{1,0:T(8,128)S(1)}, u32[]{:S(2)}, u32[]{:S(2)}) %collective-permute-start.3) | collective-permute-done | bytes 32800 | tf_op jit(solution)/shard_map/ppermute | solution.py:33
  78.3 2.9 %shard_map.127 = (f32[8,64,128]{2,1,0:T(8,128)}, f32[64,128]{1,0:T(8,128)}) custom-call(f32[9,64,128]{2,1,0:T(8,128)S(1)} %get-tuple-element.11.refs_0_, f32[8,64,128]{2,1,0:T(8,128)S(1)} %bitcast.22, f32[64,128]{1,0:T(8,128)S(1)} %bitcast.28, f32[64,128]{1,0:T(8,128)S(1)} %bitcast.31, f32[64,128]{1,0:T(8,128)S(1)} %bitcast.34, ...), custom_call_target="tpu_custom_call" | custom-call | flops 10000000 | bytes 2000000 | tf_op jit(solution)/shard_map/pallas_call | solution.py:17
  (15 shorter events, 0.0 us)
Async XLA Ops:
  0.6 1.0 %copy-start.8 = (f32[1,1,128,4]{2,3,1,0:T(4,128)S(1)}, f32[1,1,128,4]{2,3,1,0:T(4,128)}, u32[]{:S(2)}) copy-start(f32[1,1,128,4]{2,3,1,0:T(4,128)} %param.21) | copy-start | bytes 6148
  1.6 0.7 copy-start.7
  1.6 0.7 copy-start.6
  1.6 0.7 copy-start.9
  2.3 21.8 %copy-start.2 = (f32[2,32,128]{2,1,0:T(8,128)S(1)}, f32[2,32,128]{2,1,0:T(8,128)}, u32[]{:S(2)}) copy-start(f32[2,32,128]{2,1,0:T(8,128)} %param.12) | copy-start | bytes 98308
  2.3 21.8 %copy-start.3 = (f32[2,32,128]{2,1,0:T(8,128)S(1)}, f32[2,32,128]{2,1,0:T(8,128)}, u32[]{:S(2)}) copy-start(f32[2,32,128]{2,1,0:T(8,128)} %param.14) | copy-start | bytes 98308
  2.3 21.9 %copy-start.4 = (f32[2,32,128]{2,1,0:T(8,128)S(1)}, f32[2,32,128]{2,1,0:T(8,128)}, u32[]{:S(2)}) copy-start(f32[2,32,128]{2,1,0:T(8,128)} %param.15) | copy-start | bytes 98308
  3.2 21.0 %copy-start = (f32[8,2,32,128]{3,2,1,0:T(8,128)S(1)}, f32[8,2,32,128]{3,2,1,0:T(8,128)}, u32[]{:S(2)}) copy-start(f32[8,2,32,128]{3,2,1,0:T(8,128)} %param.11) | copy-start | bytes 786436
  3.2 33.9 %copy-start.1 = (bf16[8,4,2,32,128]{4,3,2,1,0:T(8,128)(2,1)S(1)}, bf16[8,4,2,32,128]{4,3,2,1,0:T(8,128)(2,1)}, u32[]{:S(2)}) copy-start(bf16[8,4,2,32,128]{4,3,2,1,0:T(8,128)(2,1)} %param.16) | copy-start | bytes 1572868
  3.2 36.7 %all-to-all-start.1 = ((bf16[128,8,128]{2,1,0:T(8,128)(2,1)}), bf16[128,8,128]{2,1,0:T(8,128)(2,1)S(1)}, u32[]{:S(2)}, u32[]{:S(2)}) async-start(bf16[128,8,128]{2,1,0:T(8,128)(2,1)} %shard_map.124), calls=%async_computation.1 | async-start | bytes 524288 | tf_op jit(solution)/shard_map/all_to_all | solution.py:274
  24.2 12.9 %copy-start.5 = (f32[2,32,128]{2,1,0:T(8,128)S(1)}, f32[2,32,128]{2,1,0:T(8,128)}, u32[]{:S(2)}) copy-start(f32[2,32,128]{2,1,0:T(8,128)} %param.13) | copy-start | bytes 98308
  24.4 12.6 %collective-permute-start = (f32[64,128]{1,0:T(8,128)S(1)}, f32[64,128]{1,0:T(8,128)S(1)}, u32[]{:S(2)}, u32[]{:S(2)}) collective-permute-start(f32[64,128]{1,0:T(8,128)S(1)} %get-tuple-element.9), channel_id=1, source_target_pairs={{0,4},{4,8},{8,12},{12,16},{16,20},{20,24},{24,28},{28,32},{32,36}... | collective-permute-start | bytes 98312 | tf_op jit(solution)/shard_map/ppermute | solution.py:33
  26.9 10.1 %collective-permute-start.1 = (f32[64,128]{1,0:T(8,128)S(1)}, f32[64,128]{1,0:T(8,128)S(1)}, u32[]{:S(2)}, u32[]{:S(2)}) collective-permute-start(f32[64,128]{1,0:T(8,128)S(1)} %get-tuple-element.10), channel_id=1, source_target_pairs={{0,508},{4,0},{8,4},{12,8},{16,12},{20,16},{24,20},{28,24},{32,28}... | collective-permute-start | bytes 98312 | tf_op jit(solution)/shard_map/ppermute | solution.py:33
  65.7 11.6 %collective-permute-start.2 = (f32[64,128]{1,0:T(8,128)S(1)}, f32[64,128]{1,0:T(8,128)S(1)}, u32[]{:S(2)}, u32[]{:S(2)}) collective-permute-start(f32[64,128]{1,0:T(8,128)S(1)} %get-tuple-element.12), channel_id=1, source_target_pairs={{0,4},{4,8},{8,12},{12,16},{16,20},{20,24},{24,28},{28,32},{32,36}... | collective-permute-start | bytes 98312 | tf_op jit(solution)/shard_map/ppermute | solution.py:33
  67.8 10.4 %collective-permute-start.3 = (f32[64,128]{1,0:T(8,128)S(1)}, f32[64,128]{1,0:T(8,128)S(1)}, u32[]{:S(2)}, u32[]{:S(2)}) collective-permute-start(f32[64,128]{1,0:T(8,128)S(1)} %get-tuple-element.13), channel_id=1, source_target_pairs={{0,508},{4,0},{8,4},{12,8},{16,12},{20,16},{24,20},{28,24},{32,28}... | collective-permute-start | bytes 98312 | tf_op jit(solution)/shard_map/ppermute | solution.py:33

commit v2 on v1

--- a/solution.py
+++ b/solution.py
@@ -31,10 +31,6 @@
 def shifted(x, axis, by):
     count = lax.axis_size(axis)
     return lax.ppermute(x, axis, [(i, (i + by) % count) for i in range(count)])
-
-
-def everyone(copies):
-    return lax.all_to_all(copies, "mem", split_axis=0, concat_axis=0, tiled=True)
 
 
 def split_two(x):
@@ -143,8 +139,7 @@
     static = (share * sigma_ref[...]) * smooth(static_ref[...], members)
     for t in range(slots):
         part = scale * total[t] + static
-        for g in range(out_ref.shape[0]):
-            out_ref[g, t * rows : (t + 1) * rows, :] = part
+        out_ref[t * rows : (t + 1) * rows, :] = part
 
 
 def observe_body(cap, parts_ref, seen_ref, out_ref):
@@ -181,8 +176,7 @@
         spread = jnp.where(hit, piece.astype(F32), 0.0).astype(BF16)
         term = jnp.dot(spread, seen, preferred_element_type=F32)
         out = term if out is None else out + term
-    for g in range(out_ref.shape[0]):
-        out_ref[g] = out
+    out_ref[...] = out
 
 
 def source_body(scale, parts_ref, pert_ref, sigma_ref, out_ref, east_ref, west_ref):
@@ -275,7 +269,7 @@
 
     partial = call(
         lambda *refs: increment_body(latitudes, scale, 1.0 / groups, *refs),
-        shape((groups, table_rows, columns)),
+        shape((table_rows, columns)),
         1e7,
         4e6,
         ens,
@@ -287,16 +281,16 @@
         west0,
         east0,
     )
-    parts = everyone(partial)
+    parts = lax.all_gather(partial, "mem")
     partial_grad = call(
         lambda *refs: observe_body(cap, *refs),
-        shape((groups, table_rows, columns)),
+        shape((table_rows, columns)),
         3e8,
         4e6,
         parts,
         seen.reshape(tiles * room, columns),
     )
-    grad_parts = everyone(partial_grad)
+    grad_parts = lax.all_gather(partial_grad, "mem")
     source, to_east, to_west = call(
         lambda *refs: source_body(scale, *refs),
         (shape((members + 1, rows, columns)), field, field),

time: 81.6 us -> 73.6 us (0.902)
  blocking collectives: 24.4 us -> 16.4 us
    all_to_all x2 -> x0, blocking collectives: 24.4 us -> none  [everyone(): lax.all_to_all(copies, 'mem', split_axis=0, concat_axis=0, tiled=True)]
    all_gather x0 -> x2, blocking collectives: none -> 16.4 us  [the longest x1 9.08 us: on_device(): parts = lax.all_gather(partial, 'mem')]
  transfers between devices with their start and end apart: 5 -> 5, of which waited for: 3 -> 2; matrix products, arithmetic and copies ran while one was open for 0% -> 0% of each run, Pallas kernels for 3% -> 3%
where the time goes in v2:
time: 73.6 us; the launch traced here: 73.2 us
  starting transfers between devices  44.7 us (61%)
  blocking collectives  16.4 us (22%)
  Pallas kernels  7.63 us (10%)
  waiting for transfers between devices  2 us (3%)
  local copies, waits for them, and re-layouts  1.66 us (2%)
  between operations  0.8 us (1%)
    ppermute x4, starting transfers between devices, shifted(): return lax.ppermute(x, axis, [(i, (i + by) % count) for i in range(count)])  23.8 us
    all_to_all x1, starting transfers between devices, on_device(): lax.all_to_all(message, 'tile', split_axis=0, concat_axis=0, tiled=True)  20.9 us
    all_gather x1, blocking collectives, on_device(): parts = lax.all_gather(partial, 'mem')  9.08 us
    pallas_call x6, Pallas kernels, call(): pl.pallas_call(body, out_shape=out, in_specs=[VMEM] * len(operands), out_...  7.63 us
    all_gather x1, blocking collectives, on_device(): grad_parts = lax.all_gather(partial_grad, 'mem')  7.29 us
    ppermute x4, waiting for transfers between devices, shifted(): return lax.ppermute(x, axis, [(i, (i + by) % count) for i in range(count)])  2 us
  transfers between devices with their start and end apart: 5, of which 2 were waited for; matrix products, arithmetic and copies ran while one was open for 0% of the time, Pallas kernels for 3%

profile of v2, /device:TPU:1, one launch (start us, length us, event | category | flops | bytes accessed | tf_op | source)
XLA Modules:
  0.0 73.2 jit_solution(14659385744287282030)
XLA Ops:
  0.6 1.0 %pad.4.fp_ref = bf16[128,8,128]{2,1,0:T(8,128)(2,1)S(1)} pad(bf16[128,4,128]{2,1,0:T(4,128)(2,1)} %bitcast.45, bf16[]{:T(256)} %constant.2.clone.1), padding=0_0x0_4x0_0 | pad | bytes 393218 | tf_op jit(solution)/shard_map/jit(_pad)/pad | solution.py:256
  1.6 0.0 copy-start.7
  1.6 0.0 copy-start.6
  1.6 0.0 copy-start.9
  1.7 0.6 copy-done.7
  2.3 0.0 copy-done.6
  2.3 0.9 %shard_map.124 = bf16[128,8,128]{2,1,0:T(8,128)(2,1)} custom-call(bf16[128,8,128]{2,1,0:T(8,128)(2,1)S(1)} %pad.4.fp_ref, s32[1,128]{1,0:T(1,128)S(1)} %bitcast.44, s32[4,128]{1,0:T(4,128)S(1)} %bitcast.41, f32[4,128]{1,0:T(4,128)S(1)} %bitcast.42, f32[4,128]{1,0:T(4,128)S(1)} %bitcast.43), custom_call_target="tpu_custom_call" | custom-call | flops 1000000 | bytes 1000000 | tf_op jit(solution)/shard_map/pallas_call | solution.py:17
  3.2 20.9 %all-to-all-start = ((bf16[128,8,128]{2,1,0:T(8,128)(2,1)}), bf16[128,8,128]{2,1,0:T(8,128)(2,1)S(1)}, u32[]{:S(2)}, u32[]{:S(2)}) async-start(bf16[128,8,128]{2,1,0:T(8,128)(2,1)} %shard_map.124), calls=%async_computation | async-start | bytes 524288 | tf_op jit(solution)/shard_map/all_to_all | solution.py:268
  24.2 0.0 copy-start.5
  24.2 0.2 shard_map.122
  24.4 2.5 %collective-permute-start = (f32[64,128]{1,0:T(8,128)S(1)}, f32[64,128]{1,0:T(8,128)S(1)}, u32[]{:S(2)}, u32[]{:S(2)}) collective-permute-start(f32[64,128]{1,0:T(8,128)S(1)} %get-tuple-element.9), channel_id=1, source_target_pairs={{0,4},{4,8},{8,12},{12,16},{16,20},{20,24},{24,28},{28,32},{32,36}... | collective-permute-start | bytes 98312 | tf_op jit(solution)/shard_map/ppermute | solution.py:33
  26.9 9.1 %collective-permute-start.1 = (f32[64,128]{1,0:T(8,128)S(1)}, f32[64,128]{1,0:T(8,128)S(1)}, u32[]{:S(2)}, u32[]{:S(2)}) collective-permute-start(f32[64,128]{1,0:T(8,128)S(1)} %get-tuple-element.10), channel_id=1, source_target_pairs={{0,508},{4,0},{8,4},{12,8},{16,12},{20,16},{24,20},{28,24},{32,28}... | collective-permute-start | bytes 98312 | tf_op jit(solution)/shard_map/ppermute | solution.py:33
  36.1 1.0 %collective-permute-done.refs_6_.refs_5_ = f32[64,128]{1,0:T(8,128)S(1)} collective-permute-done((f32[64,128]{1,0:T(8,128)S(1)}, f32[64,128]{1,0:T(8,128)S(1)}, u32[]{:S(2)}, u32[]{:S(2)}) %collective-permute-start) | collective-permute-done | bytes 32800 | tf_op jit(solution)/shard_map/ppermute | solution.py:33
  37.0 0.0 collective-permute-done.1.refs_7_.refs_6_
  37.1 2.2 %shard_map.123 = f32[256,128]{1,0:T(8,128)S(1)} custom-call(f32[8,64,128]{2,1,0:T(8,128)S(1)} %bitcast.23, f32[64,128]{1,0:T(8,128)S(1)} %bitcast.30, f32[64,128]{1,0:T(8,128)S(1)} %bitcast.39, f32[64,128]{1,0:T(8,128)S(1)} %bitcast.33, f32[64,128]{1,0:T(8,128)S(1)} %bitcast.36, bf16[8,4,64,128]{3,2,1,0:T(8,128)(2,1)S(1)} %bitcast.26, ...), custom_call_target="tpu_custom_call" | custom-call | flops 10000000 | bytes 4000000 | tf_op jit(solution)/shard_map/pallas_call | solution.py:17
  39.3 9.1 %all-gather = f32[1024,128]{1,0:T(8,128)S(1)} all-gather(f32[256,128]{1,0:T(8,128)S(1)} %shard_map.123), channel_id=2, replica_groups=mesh['tile'=128,'mem'=4] {'mem'}, dimensions={0}, use_global_device_ids=true | all-gather | bytes 655360 | tf_op jit(solution)/shard_map/all_gather | solution.py:284
  48.4 0.0 all-to-all-done
  48.4 1.2 %shard_map.125 = f32[256,128]{1,0:T(8,128)S(1)} custom-call(f32[4,256,128]{2,1,0:T(8,128)S(1)} %bitcast.28, bf16[1024,128]{1,0:T(8,128)(2,1)S(1)} %bitcast.38), custom_call_target="tpu_custom_call" | custom-call | flops 300000000 | bytes 4000000 | tf_op jit(solution)/shard_map/pallas_call | solution.py:17
  49.6 7.3 %all-gather.1 = f32[1024,128]{1,0:T(8,128)S(1)} all-gather(f32[256,128]{1,0:T(8,128)S(1)} %shard_map.125), channel_id=3, replica_groups=mesh['tile'=128,'mem'=4] {'mem'}, dimensions={0}, use_global_device_ids=true | all-gather | bytes 655360 | tf_op jit(solution)/shard_map/all_gather | solution.py:293
  56.8 0.2 shard_map.126
  57.1 1.9 %collective-permute-start.2 = (f32[64,128]{1,0:T(8,128)S(1)}, f32[64,128]{1,0:T(8,128)S(1)}, u32[]{:S(2)}, u32[]{:S(2)}) collective-permute-start(f32[64,128]{1,0:T(8,128)S(1)} %get-tuple-element.12), channel_id=1, source_target_pairs={{0,4},{4,8},{8,12},{12,16},{16,20},{20,24},{24,28},{28,32},{32,36}... | collective-permute-start | bytes 98312 | tf_op jit(solution)/shard_map/ppermute | solution.py:33
  59.0 10.3 %collective-permute-start.3 = (f32[64,128]{1,0:T(8,128)S(1)}, f32[64,128]{1,0:T(8,128)S(1)}, u32[]{:S(2)}, u32[]{:S(2)}) collective-permute-start(f32[64,128]{1,0:T(8,128)S(1)} %get-tuple-element.13), channel_id=1, source_target_pairs={{0,508},{4,0},{8,4},{12,8},{16,12},{20,16},{24,20},{28,24},{32,28}... | collective-permute-start | bytes 98312 | tf_op jit(solution)/shard_map/ppermute | solution.py:33
  69.3 1.0 %collective-permute-done.3.refs_8_ = f32[64,128]{1,0:T(8,128)S(1)} collective-permute-done((f32[64,128]{1,0:T(8,128)S(1)}, f32[64,128]{1,0:T(8,128)S(1)}, u32[]{:S(2)}, u32[]{:S(2)}) %collective-permute-start.3) | collective-permute-done | bytes 32800 | tf_op jit(solution)/shard_map/ppermute | solution.py:33
  70.3 2.9 %shard_map.127 = (f32[8,64,128]{2,1,0:T(8,128)}, f32[64,128]{1,0:T(8,128)}) custom-call(f32[9,64,128]{2,1,0:T(8,128)S(1)} %get-tuple-element.11.refs_0_, f32[8,64,128]{2,1,0:T(8,128)S(1)} %bitcast.24, f32[64,128]{1,0:T(8,128)S(1)} %bitcast.31, f32[64,128]{1,0:T(8,128)S(1)} %bitcast.34, f32[64,128]{1,0:T(8,128)S(1)} %bitcast.37, ...), custom_call_target="tpu_custom_call" | custom-call | flops 10000000 | bytes 2000000 | tf_op jit(solution)/shard_map/pallas_call | solution.py:17
  (15 shorter events, 0.0 us)
Async XLA Ops:
  0.6 1.0 %copy-start.8 = (f32[1,1,128,4]{2,3,1,0:T(4,128)S(1)}, f32[1,1,128,4]{2,3,1,0:T(4,128)}, u32[]{:S(2)}) copy-start(f32[1,1,128,4]{2,3,1,0:T(4,128)} %param.21) | copy-start | bytes 6148
  1.6 0.7 copy-start.7
  1.6 0.7 copy-start.6
  1.6 0.7 copy-start.9
  2.3 21.8 %copy-start.2 = (f32[2,32,128]{2,1,0:T(8,128)S(1)}, f32[2,32,128]{2,1,0:T(8,128)}, u32[]{:S(2)}) copy-start(f32[2,32,128]{2,1,0:T(8,128)} %param.12) | copy-start | bytes 98308
  2.3 21.8 %copy-start.3 = (f32[2,32,128]{2,1,0:T(8,128)S(1)}, f32[2,32,128]{2,1,0:T(8,128)}, u32[]{:S(2)}) copy-start(f32[2,32,128]{2,1,0:T(8,128)} %param.14) | copy-start | bytes 98308
  2.3 21.9 %copy-start.4 = (f32[2,32,128]{2,1,0:T(8,128)S(1)}, f32[2,32,128]{2,1,0:T(8,128)}, u32[]{:S(2)}) copy-start(f32[2,32,128]{2,1,0:T(8,128)} %param.15) | copy-start | bytes 98308
  3.2 21.0 %copy-start = (f32[8,2,32,128]{3,2,1,0:T(8,128)S(1)}, f32[8,2,32,128]{3,2,1,0:T(8,128)}, u32[]{:S(2)}) copy-start(f32[8,2,32,128]{3,2,1,0:T(8,128)} %param.11) | copy-start | bytes 786436
  3.2 33.9 %copy-start.1 = (bf16[8,4,2,32,128]{4,3,2,1,0:T(8,128)(2,1)S(1)}, bf16[8,4,2,32,128]{4,3,2,1,0:T(8,128)(2,1)}, u32[]{:S(2)}) copy-start(bf16[8,4,2,32,128]{4,3,2,1,0:T(8,128)(2,1)} %param.16) | copy-start | bytes 1572868
  3.2 45.2 %all-to-all-start = ((bf16[128,8,128]{2,1,0:T(8,128)(2,1)}), bf16[128,8,128]{2,1,0:T(8,128)(2,1)S(1)}, u32[]{:S(2)}, u32[]{:S(2)}) async-start(bf16[128,8,128]{2,1,0:T(8,128)(2,1)} %shard_map.124), calls=%async_computation | async-start | bytes 524288 | tf_op jit(solution)/shard_map/all_to_all | solution.py:268
  24.2 12.9 %copy-start.5 = (f32[2,32,128]{2,1,0:T(8,128)S(1)}, f32[2,32,128]{2,1,0:T(8,128)}, u32[]{:S(2)}) copy-start(f32[2,32,128]{2,1,0:T(8,128)} %param.13) | copy-start | bytes 98308
  24.4 12.6 %collective-permute-start = (f32[64,128]{1,0:T(8,128)S(1)}, f32[64,128]{1,0:T(8,128)S(1)}, u32[]{:S(2)}, u32[]{:S(2)}) collective-permute-start(f32[64,128]{1,0:T(8,128)S(1)} %get-tuple-element.9), channel_id=1, source_target_pairs={{0,4},{4,8},{8,12},{12,16},{16,20},{20,24},{24,28},{28,32},{32,36}... | collective-permute-start | bytes 98312 | tf_op jit(solution)/shard_map/ppermute | solution.py:33
  26.9 10.1 %collective-permute-start.1 = (f32[64,128]{1,0:T(8,128)S(1)}, f32[64,128]{1,0:T(8,128)S(1)}, u32[]{:S(2)}, u32[]{:S(2)}) collective-permute-start(f32[64,128]{1,0:T(8,128)S(1)} %get-tuple-element.10), channel_id=1, source_target_pairs={{0,508},{4,0},{8,4},{12,8},{16,12},{20,16},{24,20},{28,24},{32,28}... | collective-permute-start | bytes 98312 | tf_op jit(solution)/shard_map/ppermute | solution.py:33
  57.1 12.2 %collective-permute-start.2 = (f32[64,128]{1,0:T(8,128)S(1)}, f32[64,128]{1,0:T(8,128)S(1)}, u32[]{:S(2)}, u32[]{:S(2)}) collective-permute-start(f32[64,128]{1,0:T(8,128)S(1)} %get-tuple-element.12), channel_id=1, source_target_pairs={{0,4},{4,8},{8,12},{12,16},{16,20},{20,24},{24,28},{28,32},{32,36}... | collective-permute-start | bytes 98312 | tf_op jit(solution)/shard_map/ppermute | solution.py:33
  59.0 11.3 %collective-permute-start.3 = (f32[64,128]{1,0:T(8,128)S(1)}, f32[64,128]{1,0:T(8,128)S(1)}, u32[]{:S(2)}, u32[]{:S(2)}) collective-permute-start(f32[64,128]{1,0:T(8,128)S(1)} %get-tuple-element.13), channel_id=1, source_target_pairs={{0,508},{4,0},{8,4},{12,8},{16,12},{20,16},{24,20},{28,24},{32,28}... | collective-permute-start | bytes 98312 | tf_op jit(solution)/shard_map/ppermute | solution.py:33

commit v3 on v2

v3 whole, which is shorter than its diff:
```python
import math

import jax
import jax.numpy as jnp
from jax import lax
from jax.experimental import pallas as pl
from jax.experimental.pallas import tpu as pltpu
from jax.sharding import PartitionSpec as P

SWEEPS = 2
F32 = jnp.float32
BF16 = jnp.bfloat16
BESIDE = 1e9
RUN = 4
VMEM = pl.BlockSpec(memory_space=pltpu.VMEM)
BLOCKS = pl.BlockSpec()


def call(body, out, flops, traffic, *operands, spec=VMEM, limit=32):
    return pl.pallas_call(
        body,
        out_shape=out,
        in_specs=[spec] * len(operands),
        out_specs=jax.tree.map(lambda _: VMEM, out),
        cost_estimate=pl.CostEstimate(flops=int(flops), bytes_accessed=int(traffic), transcendentals=0),
        compiler_params=pltpu.CompilerParams(vmem_limit_bytes=limit * 1024 * 1024),
    )(*operands)


def shape(dims, kind=F32):
    return jax.ShapeDtypeStruct(dims, kind)


def from_neighbours(x, axis):
    count = lax.axis_size(axis)
    swaps = []
    for start in (1, 0):
        pairs = [(i % count, (i + 1) % count) for i in range(start, count + start, 2)]
        swaps.append(lax.ppermute(x, axis, pairs + [(j, i) for i, j in pairs]))
    odd = lax.axis_index(axis) % 2 == 1
    return jnp.where(odd, swaps[1], swaps[0]), jnp.where(odd, swaps[0], swaps[1])


def spread(x, axis):
    count = lax.axis_size(axis)
    inner, outer = x.shape[:2]
    runs = [[o * inner + i for i in range(inner)] for o in range(outer)]
    across = [[o * inner + i for o in range(outer)] for i in range(inner)]
    x = lax.all_to_all(x, axis, 0, 0, axis_index_groups=runs, tiled=True)
    x = jnp.swapaxes(x, 0, 1)
    x = lax.all_to_all(x, axis, 0, 0, axis_index_groups=across, tiled=True)
    return x.reshape(count, *x.shape[2:])


def split_two(x):
    high = x.astype(BF16)
    return high, (x - high.astype(F32)).astype(BF16)


def split_three(x):
    high = x.astype(BF16)
    rest = x - high.astype(F32)
    mid = rest.astype(BF16)
    return high, mid, (rest - mid.astype(F32)).astype(BF16)


WIDE = 12
EDGE = 2


def lanes_of(dims):
    return lax.broadcasted_iota(jnp.int32, dims, 1)


def turn(x, by):
    by = by % x.shape[1]
    return pltpu.roll(x, by, 1) if by else x


def between(lane, low, high):
    return (lane >= low) & (lane < high)


def own_edges(x, start, keep, lane, packed):
    columns = x.shape[1]
    packed = jnp.where(between(lane, start, start + keep), turn(x, start), packed)
    end = start + 2 * keep
    return jnp.where(between(lane, start + keep, end), turn(x, end - columns), packed)


def pack_fields(fields):
    packed = jnp.zeros(fields[0].shape, F32)
    lane = lanes_of(packed.shape)
    for f, u in enumerate(fields):
        packed = own_edges(u, WIDE * f + EDGE, WIDE // 2 - EDGE, lane, packed)
    return packed


def place_edges(packed, f, lane):
    columns = packed.shape[1]
    start = WIDE * f + EDGE
    left = turn(packed, -start)
    right = turn(packed, columns - (WIDE * (f + 1) - EDGE))
    return jnp.where(lane < EDGE, left, right)


def at_edge(lane, columns):
    return (lane < EDGE) | (lane >= columns - EDGE)


def diffuse(u, e, n):
    rows = u.shape[0]
    flux = e * (turn(u, -1) - u)
    up = n * (pltpu.roll(u, rows - 1, 0) - u)
    return u + ((flux - turn(flux, 1)) + (up - pltpu.roll(up, 1, 0)))


def smooth(u, e, n):
    for _ in range(SWEEPS):
        u = diffuse(u, e, n)
    return u


def closed(n, latitudes):
    row = lax.broadcasted_iota(jnp.int32, n.shape, 0)
    return jnp.where((row & (latitudes - 1)) == latitudes - 1, 0.0, n)


def with_neighbours(own, from_west, from_east, fields, lane):
    at = lane % WIDE
    west = (at < EDGE) & (lane < WIDE * fields)
    east = (at >= WIDE - EDGE) & (lane < WIDE * fields)
    out = jnp.where(west, turn(from_west, 2 * EDGE - WIDE), own)
    return jnp.where(east, turn(from_east, WIDE - 2 * EDGE), out)


def repeated(first, count, lane):
    out, have = first, 1
    while have < count:
        out = jnp.where(lane < WIDE * have, out, turn(out, WIDE * have))
        have *= 2
    return out


def edges_body(ens_ref, static_ref, e_ref, n_ref, out_ref):
    members = ens_ref.shape[0]
    packed = pack_fields([ens_ref[m] for m in range(members)] + [static_ref[...], e_ref[...]])
    start = WIDE * (members + 2)
    out_ref[...] = own_edges(n_ref[...], start, EDGE, lanes_of(packed.shape), packed)


def message_body(fp_ref, counts_ref, rows_ref, values_ref, precision_ref, out_ref):
    cap, dests = rows_ref.shape
    slot = lax.broadcasted_iota(jnp.int32, (cap, dests), 0)
    live = slot < counts_ref[...]
    items = [rows_ref[...].astype(F32)]
    items += [x.astype(F32) for x in split_three(values_ref[...])]
    items += [x.astype(F32) for x in split_three(jnp.where(live, precision_ref[...], 0.0))]
    items += [jnp.zeros((cap, dests), F32)]
    stacked = [x[c : c + 1] for c in range(cap) for x in items]
    stacked.append(jnp.zeros((out_ref.shape[3] - len(stacked), dests), F32))
    meta = jnp.concatenate(stacked, axis=0).T
    place = lax.broadcasted_iota(jnp.int32, (dests, *out_ref.shape[2:]), 1)
    fp = fp_ref[...].astype(F32)
    fp = jnp.concatenate([fp, jnp.zeros_like(fp)], axis=1)
    full = jnp.where(place == cap, meta[:, None, :], fp).astype(BF16)
    inner, outer = out_ref.shape[:2]
    full = full.reshape(outer, inner, *full.shape[1:])
    for i in range(inner):
        out_ref[i] = full[:, i]


def first_body(fp_ref, counts_ref, rows_ref, values_ref, precision_ref, ens_ref, static_ref, e_ref, n_ref, out_ref, own_ref):
    edges_body(ens_ref, static_ref, e_ref, n_ref, own_ref)
    message_body(fp_ref, counts_ref, rows_ref, values_ref, precision_ref, out_ref)


def inner_increment_body(latitudes, scale, share, ens_ref, static_ref, sigma_ref, e_ref, n_ref, pert_ref, out_ref):
    members, slots = pert_ref.shape[:2]
    rows, columns = e_ref.shape
    edge = at_edge(lanes_of(e_ref.shape), columns)
    e, n = e_ref[...], closed(n_ref[...], latitudes)
    total = [jnp.zeros(e_ref.shape, F32) for _ in range(slots)]
    for m in range(members):
        u = smooth(ens_ref[m], e, n)
        for t in range(slots):
            total[t] = total[t] + pert_ref[m, t].astype(F32) * u
    static = (share * sigma_ref[...]) * smooth(static_ref[...], e, n)
    for t in range(slots):
        out_ref[t * rows : (t + 1) * rows, :] = jnp.where(edge, 0.0, scale * total[t] + static)


def outer_increment_body(
    latitudes, scale, share, inner_ref, own_ref, west_ref, east_ref, sigma_ref, e_ref, n_ref, pert_ref, out_ref, e_out, n_out
):
    members, slots = pert_ref.shape[:2]
    rows, columns = e_ref.shape
    fields = members + 1
    lane = lanes_of(e_ref.shape)
    own, from_west, from_east = own_ref[...], west_ref[...], east_ref[...]

    def coefficient(x, west, west_at, east, east_at):
        first = own_edges(x, EDGE, WIDE // 2 - EDGE, lane, jnp.zeros(x.shape, F32))
        first = jnp.where(lane < EDGE, turn(west, -west_at), first)
        ends = WIDE - EDGE
        first = jnp.where(between(lane, ends, WIDE), turn(east, ends - east_at), first)
        return repeated(first, fields, lane)

    e_at, n_at = WIDE * fields, WIDE * (fields + 1)
    e = coefficient(e_ref[...], from_west, e_at + WIDE - 2 * EDGE, from_east, e_at + EDGE)
    n = coefficient(n_ref[...], from_west, n_at + EDGE, from_east, n_at)
    n = closed(n, latitudes)
    e_out[...] = e
    n_out[...] = n
    packed = smooth(with_neighbours(own, from_west, from_east, fields, lane), e, n)
    total = [jnp.zeros(e_ref.shape, F32) for _ in range(slots)]
    for m in range(members):
        u = place_edges(packed, m, lane)
        for t in range(slots):
            total[t] = total[t] + pert_ref[m, t].astype(F32) * u
    static = (share * sigma_ref[...]) * place_edges(packed, members, lane)
    edge = at_edge(lane, columns)
    for t in range(slots):
        span = slice(t * rows, (t + 1) * rows)
        out_ref[span, :] = jnp.where(edge, scale * total[t] + static, inner_ref[span, :])


def observe_body(cap, parts_ref, seen_ref, out_ref):
    table = parts_ref[0]
    for g in range(1, parts_ref.shape[0]):
        table = table + parts_ref[g]
    rows, columns = table.shape
    high, low = split_two(table)
    seen = seen_ref[...]
    count = seen.shape[0]
    room = seen.shape[0] // seen_ref.shape[0]
    group = 8
    eye_shape = (group * cap, columns)
    eye = (
        lax.broadcasted_iota(jnp.int32, eye_shape, 0) == lax.broadcasted_iota(jnp.int32, eye_shape, 1)
    ).astype(F32).astype(BF16)
    contract = (((1,), (1,)), ((), ()))
    got = lax.dot_general(high, seen, contract, preferred_element_type=F32)
    got = got + lax.dot_general(low, seen, contract, preferred_element_type=F32)
    meta = lax.dot_general(eye, seen, contract, preferred_element_type=F32)
    place = lax.broadcasted_iota(jnp.int32, (group, count), 1) & (group - 1)
    facts = jnp.zeros((group, count), F32)
    for c in range(cap):
        part = pltpu.roll(meta[c * group : (c + 1) * group], count - (cap - c), 1)
        facts = jnp.where(place == c, part, facts)
    row_of = jnp.where(place[:1] < cap, facts[0:1], -1.0).astype(jnp.int32)
    value = (facts[1:2] + facts[2:3]) + facts[3:4]
    precision = (facts[4:5] + facts[5:6]) + facts[6:7]
    hit = lax.broadcasted_iota(jnp.int32, (rows, count), 0) == row_of
    model = jnp.sum(jnp.where(hit, got, 0.0), axis=0, keepdims=True)
    residual = precision * (model - value)
    out = None
    for piece in split_two(residual):
        spread = jnp.where(hit, piece.astype(F32), 0.0).astype(BF16)
        term = jnp.dot(spread, seen, preferred_element_type=F32)
        out = term if out is None else out + term
    out_ref[...] = out


def source_body(scale, parts_ref, pert_ref, sigma_ref, out_ref, packed_ref):
    members, slots, rows = pert_ref.shape[:3]
    gradient = []
    for t in range(slots):
        span = slice(t * rows, (t + 1) * rows)
        g = parts_ref[0, span, :]
        for k in range(1, parts_ref.shape[0]):
            g = g + parts_ref[k, span, :]
        gradient.append(g)
    fields = []
    for m in range(members):
        u = pert_ref[m, 0].astype(F32) * gradient[0]
        for t in range(1, slots):
            u = u + pert_ref[m, t].astype(F32) * gradient[t]
        u = scale * u
        out_ref[m] = u
        fields.append(u)
    u = gradient[0]
    for t in range(1, slots):
        u = u + gradient[t]
    u = sigma_ref[...] * u
    out_ref[members] = u
    packed_ref[...] = pack_fields(fields + [u])


def inner_result_body(latitudes, source_ref, ens_ref, static_ref, e_ref, n_ref, out_ref):
    members = ens_ref.shape[0]
    e, n = e_ref[...], closed(n_ref[...], latitudes)
    for f in range(members + 1):
        out_ref[f] = smooth(source_ref[f], e, n) + (ens_ref[f] if f < members else static_ref[...])


def outer_result_body(inner_ref, own_ref, west_ref, east_ref, controls_ref, e_ref, n_ref, ens_out, static_out):
    members, _, columns = ens_out.shape
    lane = lanes_of(own_ref.shape)
    edge = at_edge(lane, columns)
    packed = with_neighbours(own_ref[...], west_ref[...], east_ref[...], members + 1, lane)
    packed = smooth(packed, e_ref[...], n_ref[...]) + controls_ref[...]
    for f in range(members + 1):
        u = jnp.where(edge, place_edges(packed, f, lane), inner_ref[f])
        if f < members:
            ens_out[f] = u
        else:
            static_out[...] = u


def on_device(
    control_ens,
    control_static,
    static_sigma,
    east_coef,
    north_coef,
    perturbations,
    obs_counts,
    obs_rows,
    footprints,
    obs_values,
    obs_precision,
):
    members, levels, latitudes, columns = control_ens.shape
    slots = perturbations.shape[1]
    rows = levels * latitudes
    table_rows = slots * rows
    groups = lax.axis_size("mem")
    scale = 1.0 / math.sqrt(members * groups - 1)
    ens = control_ens.reshape(members, rows, columns)
    static = control_static.reshape(rows, columns)
    sigma = static_sigma.reshape(rows, columns)
    e = east_coef.reshape(rows, columns)
    n = north_coef.reshape(rows, columns)
    pert = perturbations.reshape(members, slots, rows, columns)
    tiles, cap = obs_rows.shape[2:]

    field = shape((rows, columns))

    room = 8
    message, own = call(
        first_body,
        (shape((RUN, tiles // RUN, room, columns), BF16), field),
        1e6,
        1e6,
        footprints[0, 0],
        obs_counts[0],
        obs_rows[0, 0].T,
        obs_values[0, 0].T,
        obs_precision[0, 0].T,
        ens,
        static,
        e,
        n,
        spec=BLOCKS,
        limit=60,
    )
    west, east = from_neighbours(own, "tile")
    seen = spread(message, "tile")

    share = 1.0 / groups
    inner = call(
        lambda *refs: inner_increment_body(latitudes, scale, share, *refs),
        shape((table_rows, columns)),
        BESIDE,
        4e6,
        ens,
        static,
        sigma,
        e,
        n,
        pert,
    )
    partial, e_packed, n_packed = call(
        lambda *refs: outer_increment_body(latitudes, scale, share, *refs),
        (shape((table_rows, columns)), field, field),
        1e7,
        4e6,
        inner,
        own,
        west,
        east,
        sigma,
        e,
        n,
        pert,
    )
    parts = lax.all_gather(partial, "mem")
    partial_grad = call(
        lambda *refs: observe_body(cap, *refs),
        shape((table_rows, columns)),
        3e8,
        4e6,
        parts,
        seen.reshape(tiles * room, columns),
    )
    grad_parts = lax.all_gather(partial_grad, "mem")
    source, own_source = call(
        lambda *refs: source_body(scale, *refs),
        (shape((members + 1, rows, columns)), field),
        1e7,
        2e6,
        grad_parts,
        pert,
        sigma,
    )
    west, east = from_neighbours(own_source, "tile")
    inner = call(
        lambda *refs: inner_result_body(latitudes, *refs),
        shape(source.shape),
        BESIDE,
        4e6,
        source,
        ens,
        static,
        e,
        n,
    )
    ens_out, static_out = call(
        outer_result_body,
        (shape(ens.shape), field),
        1e7,
        2e6,
        inner,
        own_source,
        west,
        east,
        own,
        e_packed,
        n_packed,
    )
    return ens_out.reshape(control_ens.shape), static_out.reshape(control_static.shape)


def solution(mesh):
    placed = (
        P("mem", None, None, "tile"),
        P(None, None, "tile"),
        P(None, None, "tile"),
        P(None, None, "tile"),
        P(None, None, "tile"),
        P("mem", None, None, None, "tile"),
        P("mem", "tile", None),
        P("mem", "tile", None, None),
        P("mem", "tile", None, None, None),
        P("mem", "tile", None, None),
        P("mem", "tile", None, None),
    )
    return jax.shard_map(
        on_device,
        mesh=mesh,
        in_specs=placed,
        out_specs=(P("mem", None, None, "tile"), P(None, None, "tile")),
        check_vma=False,
    )
```

time: 73.6 us -> 67.6 us (0.918)
  starting transfers between devices: 44.7 us -> 35.8 us
  blocking collectives: 16.4 us -> 20.6 us
  Pallas kernels: 7.63 us -> 6.64 us
  local copies, waits for them, and re-layouts: 1.66 us -> 0.78 us
    all_to_all x1 -> x2, starting transfers between devices: 20.9 us -> 9.42 us  [the longest x1 4.97 us: spread(): x = lax.all_to_all(x, axis, 0, 0, axis_index_groups=runs, tiled=True)]
    all_gather x1, blocking collectives: 9.08 us -> 12.7 us  [on_device(): parts = lax.all_gather(partial, 'mem')]
    ppermute x4, starting transfers between devices: 23.8 us -> 26.4 us  [from_neighbours(): swaps.append(lax.ppermute(x, axis, pairs + [(j, i) for i, j in pairs]))]
    pallas_call x6 -> x7, Pallas kernels: 7.63 us -> 6.64 us  [call(): pl.pallas_call(body, out_shape=out, in_specs=[spec] * len(operands), out_...]
    pad x1 -> x0, local copies, waits for them, and re-layouts: 0.96 us -> none  [on_device(): padded = jnp.pad(footprints[0, 0], ((0, 0), (0, room - cap), (0, 0)))]
    transpose x0 -> x1, local copies, waits for them, and re-layouts: none -> 0.75 us  [spread(): x = jnp.swapaxes(x, 0, 1)]
  transfers between devices with their start and end apart: 5 -> 6, of which waited for: 2 -> 2; matrix products, arithmetic and copies ran while one was open for 0% -> 1% of each run, Pallas kernels for 3% -> 3%
where the time goes in v3:
time: 67.6 us; the launch traced here: 67.1 us
  starting transfers between devices  35.8 us (53%)
  blocking collectives  20.6 us (30%)
  Pallas kernels  6.64 us (10%)
  waiting for transfers between devices  2.48 us (4%)
  between operations  0.83 us (1%)
  local copies, waits for them, and re-layouts  0.78 us (1%)
    ppermute x4, starting transfers between devices, from_neighbours(): swaps.append(lax.ppermute(x, axis, pairs + [(j, i) for i, j in pairs]))  26.4 us
    all_gather x1, blocking collectives, on_device(): parts = lax.all_gather(partial, 'mem')  12.7 us
    all_gather x1, blocking collectives, on_device(): grad_parts = lax.all_gather(partial_grad, 'mem')  7.9 us
    pallas_call x7, Pallas kernels, call(): pl.pallas_call(body, out_shape=out, in_specs=[spec] * len(operands), out_...  6.64 us
    all_to_all x1, starting transfers between devices, spread(): x = lax.all_to_all(x, axis, 0, 0, axis_index_groups=runs, tiled=True)  4.97 us
    all_to_all x1, starting transfers between devices, spread(): x = lax.all_to_all(x, axis, 0, 0, axis_index_groups=across, tiled=True)  4.45 us
    ppermute x4, waiting for transfers between devices, from_neighbours(): swaps.append(lax.ppermute(x, axis, pairs + [(j, i) for i, j in pairs]))  2.48 us
  transfers between devices with their start and end apart: 6, of which 2 were waited for; matrix products, arithmetic and copies ran while one was open for 1% of the time, Pallas kernels for 3%

profile of v3, /device:TPU:1, one launch (start us, length us, event | category | flops | bytes accessed | tf_op | source)
XLA Modules:
  0.0 67.1 jit_solution(8148160991006969809)
XLA Ops:
  0.6 2.0 %shard_map.123 = (bf16[4,32,8,128]{3,2,1,0:T(8,128)(2,1)}, f32[64,128]{1,0:T(8,128)}) custom-call(bf16[128,4,128]{2,1,0:T(4,128)(2,1)} %bitcast.47, s32[1,128]{1,0:T(1,128)} %bitcast.51, s32[4,128]{1,0:T(4,128)} %bitcast.48, f32[4,128]{1,0:T(4,128)} %bitcast.49, f32[4,128]{1,0:T(4,128)} %bitcast.50, f32[8,64,128]{2,1,0:T(8,128)} %bitcast.28, ...), custom_call_target="tpu_custom_call" | custom-call | flops 1000000 | bytes 1000000 | tf_op jit(solution)/shard_map/pallas_call | solution.py:20
  2.6 5.0 %all-to-all-start = ((bf16[4,32,8,128]{3,2,1,0:T(8,128)(2,1)}), bf16[4,32,8,128]{3,2,1,0:T(8,128)(2,1)S(1)}, u32[]{:S(2)}, u32[]{:S(2)}) async-start(bf16[4,32,8,128]{3,2,1,0:T(8,128)(2,1)} %get-tuple-element.13), calls=%async_computation | async-start | bytes 524288 | tf_op jit(solution)/shard_map/all_to_all | solution.py:49
  7.6 15.9 %collective-permute-start.1 = (f32[64,128]{1,0:T(8,128)S(1)}, f32[64,128]{1,0:T(8,128)S(1)}, u32[]{:S(2)}, u32[]{:S(2)}) collective-permute-start(f32[64,128]{1,0:T(8,128)S(1)} %copy-done.5), channel_id=1, source_target_pairs={{4,8},{12,16},{20,24},{28,32},{36,40},{44,48},{52,56},{60,64},{68,... | collective-permute-start | bytes 98312 | tf_op jit(solution)/shard_map/ppermute | solution.py:39
  23.5 1.9 %collective-permute-start = (f32[64,128]{1,0:T(8,128)S(1)}, f32[64,128]{1,0:T(8,128)S(1)}, u32[]{:S(2)}, u32[]{:S(2)}) collective-permute-start(f32[64,128]{1,0:T(8,128)S(1)} %copy-done.5), channel_id=1, source_target_pairs={{0,4},{8,12},{16,20},{24,28},{32,36},{40,44},{48,52},{56,60},{64,6... | collective-permute-start | bytes 98312 | tf_op jit(solution)/shard_map/ppermute | solution.py:39
  25.4 0.0 all-to-all-done
  25.5 0.0 copy-start
  25.5 0.7 %copy.14 = bf16[32,4,8,128]{3,2,1,0:T(8,128)(2,1)} copy(bf16[32,4,8,128]{3,2,0,1:T(8,128)(2,1)S(1)} %bitcast.46) | data formatting | bytes 524288 | tf_op jit(solution)/shard_map/transpose | solution.py:50
  26.2 0.0 copy-start.6
  26.2 4.5 %all-to-all-start.1 = ((bf16[32,4,8,128]{3,2,1,0:T(8,128)(2,1)}), bf16[32,4,8,128]{3,2,1,0:T(8,128)(2,1)S(1)}, u32[]{:S(2)}, u32[]{:S(2)}) async-start(bf16[32,4,8,128]{3,2,1,0:T(8,128)(2,1)} %copy.14), calls=%async_computation.1 | async-start | bytes 524288 | tf_op jit(solution)/shard_map/all_to_all | solution.py:51
  30.8 0.6 shard_map.122.refs_0_
  31.4 0.0 collective-permute-done.1
  31.4 0.0 collective-permute-done
  31.4 0.9 %shard_map.124 = (f32[256,128]{1,0:T(8,128)S(1)}, f32[64,128]{1,0:T(8,128)S(1)}, f32[64,128]{1,0:T(8,128)S(1)}) custom-call(f32[256,128]{1,0:T(8,128)S(1)} %shard_map.122.refs_0_, f32[64,128]{1,0:T(8,128)S(1)} %copy-done.5, f32[64,128]{1,0:T(8,128)S(1)} %get-tuple-element.23.refs_2_, f32[64,128]{1,0:T(8,128)S(1)} %get-tuple-element.22.refs_3_, ...), custom_call_target="tpu_custom_call" | custom-call | flops 10000000 | bytes 4000000 | tf_op jit(solution)/shard_map/pallas_call | solution.py:20
  32.3 12.7 %all-gather = f32[1024,128]{1,0:T(8,128)S(1)} all-gather(f32[256,128]{1,0:T(8,128)S(1)} %get-tuple-element.12), channel_id=2, replica_groups=mesh['tile'=128,'mem'=4] {'mem'}, dimensions={0}, use_global_device_ids=true | all-gather | bytes 655360 | tf_op jit(solution)/shard_map/all_gather | solution.py:388
  44.9 0.0 all-to-all-done.1
  44.9 1.2 %shard_map.125 = f32[256,128]{1,0:T(8,128)S(1)} custom-call(f32[4,256,128]{2,1,0:T(8,128)S(1)} %bitcast.27, bf16[1024,128]{1,0:T(8,128)(2,1)S(1)} %bitcast.31), custom_call_target="tpu_custom_call" | custom-call | flops 300000000 | bytes 4000000 | tf_op jit(solution)/shard_map/pallas_call | solution.py:20
  46.1 7.9 %all-gather.1 = f32[1024,128]{1,0:T(8,128)S(1)} all-gather(f32[256,128]{1,0:T(8,128)S(1)} %shard_map.125), channel_id=3, replica_groups=mesh['tile'=128,'mem'=4] {'mem'}, dimensions={0}, use_global_device_ids=true | all-gather | bytes 655360 | tf_op jit(solution)/shard_map/all_gather | solution.py:397
  54.0 0.3 shard_map.126
  54.3 6.6 %collective-permute-start.3 = (f32[64,128]{1,0:T(8,128)S(1)}, f32[64,128]{1,0:T(8,128)S(1)}, u32[]{:S(2)}, u32[]{:S(2)}) collective-permute-start(f32[64,128]{1,0:T(8,128)S(1)} %get-tuple-element.15.own_ref), channel_id=1, source_target_pairs={{4,8},{12,16},{20,24},{28,32},{36,40},{44,48},{52,56},{60,64},{68,... | collective-permute-start | bytes 98312 | tf_op jit(solution)/shard_map/ppermute | solution.py:39
  60.9 1.9 %collective-permute-start.2 = (f32[64,128]{1,0:T(8,128)S(1)}, f32[64,128]{1,0:T(8,128)S(1)}, u32[]{:S(2)}, u32[]{:S(2)}) collective-permute-start(f32[64,128]{1,0:T(8,128)S(1)} %get-tuple-element.15.own_ref), channel_id=1, source_target_pairs={{0,4},{8,12},{16,20},{24,28},{32,36},{40,44},{48,52},{56,60},{64,6... | collective-permute-start | bytes 98312 | tf_op jit(solution)/shard_map/ppermute | solution.py:39
  62.8 0.5 shard_map.127.inner_ref
  63.3 2.2 %collective-permute-done.3 = f32[64,128]{1,0:T(8,128)S(1)} collective-permute-done((f32[64,128]{1,0:T(8,128)S(1)}, f32[64,128]{1,0:T(8,128)S(1)}, u32[]{:S(2)}, u32[]{:S(2)}) %collective-permute-start.3) | collective-permute-done | bytes 32800 | tf_op jit(solution)/shard_map/ppermute | solution.py:39
  65.6 0.2 collective-permute-done.2
  65.8 1.3 %shard_map.128 = (f32[8,64,128]{2,1,0:T(8,128)}, f32[64,128]{1,0:T(8,128)}) custom-call(f32[9,64,128]{2,1,0:T(8,128)S(1)} %shard_map.127.inner_ref, f32[64,128]{1,0:T(8,128)S(1)} %get-tuple-element.15.own_ref, f32[64,128]{1,0:T(8,128)S(1)} %get-tuple-element.21.west_ref, f32[64,128]{1,0:T(8,128)S(1)} %get-tuple-element.20.east_ref, f32[64,128]{1,0:T(8,128)S(1)} %copy-done.5, ...), custom_call_target="tpu_custom_call" | custom-call | flops 10000000 | bytes 2000000 | tf_op jit(solution)/shard_map/pallas_call | solution.py:20
  (14 shorter events, 0.0 us)
Async XLA Ops:
  2.6 5.0 %copy-start.5 = (f32[64,128]{1,0:T(8,128)S(1)}, f32[64,128]{1,0:T(8,128)}, u32[]{:S(2)}) copy-start(f32[64,128]{1,0:T(8,128)} %get-tuple-element.11.refs_1_.controls_ref) | copy-start | bytes 98308
  2.6 22.9 %all-to-all-start = ((bf16[4,32,8,128]{3,2,1,0:T(8,128)(2,1)}), bf16[4,32,8,128]{3,2,1,0:T(8,128)(2,1)S(1)}, u32[]{:S(2)}, u32[]{:S(2)}) async-start(bf16[4,32,8,128]{3,2,1,0:T(8,128)(2,1)} %get-tuple-element.13), calls=%async_computation | async-start | bytes 524288 | tf_op jit(solution)/shard_map/all_to_all | solution.py:49
  7.6 23.8 %collective-permute-start.1 = (f32[64,128]{1,0:T(8,128)S(1)}, f32[64,128]{1,0:T(8,128)S(1)}, u32[]{:S(2)}, u32[]{:S(2)}) collective-permute-start(f32[64,128]{1,0:T(8,128)S(1)} %copy-done.5), channel_id=1, source_target_pairs={{4,8},{12,16},{20,24},{28,32},{36,40},{44,48},{52,56},{60,64},{68,... | collective-permute-start | bytes 98312 | tf_op jit(solution)/shard_map/ppermute | solution.py:39
  23.5 7.9 %collective-permute-start = (f32[64,128]{1,0:T(8,128)S(1)}, f32[64,128]{1,0:T(8,128)S(1)}, u32[]{:S(2)}, u32[]{:S(2)}) collective-permute-start(f32[64,128]{1,0:T(8,128)S(1)} %copy-done.5), channel_id=1, source_target_pairs={{0,4},{8,12},{16,20},{24,28},{32,36},{40,44},{48,52},{56,60},{64,6... | collective-permute-start | bytes 98312 | tf_op jit(solution)/shard_map/ppermute | solution.py:39
  25.5 5.2 %copy-start = (bf16[8,4,2,32,128]{4,3,2,1,0:T(8,128)(2,1)S(1)}, bf16[8,4,2,32,128]{4,3,2,1,0:T(8,128)(2,1)}, u32[]{:S(2)}) copy-start(bf16[8,4,2,32,128]{4,3,2,1,0:T(8,128)(2,1)} %param.16) | copy-start | bytes 1572868
  26.2 4.5 %copy-start.1 = (f32[8,2,32,128]{3,2,1,0:T(8,128)S(1)}, f32[8,2,32,128]{3,2,1,0:T(8,128)}, u32[]{:S(2)}) copy-start(f32[8,2,32,128]{3,2,1,0:T(8,128)} %param.11) | copy-start | bytes 786436
  26.2 4.5 %copy-start.2 = (f32[2,32,128]{2,1,0:T(8,128)S(1)}, f32[2,32,128]{2,1,0:T(8,128)}, u32[]{:S(2)}) copy-start(f32[2,32,128]{2,1,0:T(8,128)} %param.13) | copy-start | bytes 98308
  26.2 4.5 %copy-start.3 = (f32[2,32,128]{2,1,0:T(8,128)S(1)}, f32[2,32,128]{2,1,0:T(8,128)}, u32[]{:S(2)}) copy-start(f32[2,32,128]{2,1,0:T(8,128)} %param.14) | copy-start | bytes 98308
  26.2 4.5 %copy-start.4 = (f32[2,32,128]{2,1,0:T(8,128)S(1)}, f32[2,32,128]{2,1,0:T(8,128)}, u32[]{:S(2)}) copy-start(f32[2,32,128]{2,1,0:T(8,128)} %param.15) | copy-start | bytes 98308
  26.2 4.5 %copy-start.6 = (f32[2,32,128]{2,1,0:T(8,128)S(1)}, f32[2,32,128]{2,1,0:T(8,128)}, u32[]{:S(2)}) copy-start(f32[2,32,128]{2,1,0:T(8,128)} %param.12) | copy-start | bytes 98308
  26.2 18.7 %all-to-all-start.1 = ((bf16[32,4,8,128]{3,2,1,0:T(8,128)(2,1)}), bf16[32,4,8,128]{3,2,1,0:T(8,128)(2,1)S(1)}, u32[]{:S(2)}, u32[]{:S(2)}) async-start(bf16[32,4,8,128]{3,2,1,0:T(8,128)(2,1)} %copy.14), calls=%async_computation.1 | async-start | bytes 524288 | tf_op jit(solution)/shard_map/all_to_all | solution.py:51
  54.3 11.3 %collective-permute-start.3 = (f32[64,128]{1,0:T(8,128)S(1)}, f32[64,128]{1,0:T(8,128)S(1)}, u32[]{:S(2)}, u32[]{:S(2)}) collective-permute-start(f32[64,128]{1,0:T(8,128)S(1)} %get-tuple-element.15.own_ref), channel_id=1, source_target_pairs={{4,8},{12,16},{20,24},{28,32},{36,40},{44,48},{52,56},{60,64},{68,... | collective-permute-start | bytes 98312 | tf_op jit(solution)/shard_map/ppermute | solution.py:39
  60.9 5.0 %collective-permute-start.2 = (f32[64,128]{1,0:T(8,128)S(1)}, f32[64,128]{1,0:T(8,128)S(1)}, u32[]{:S(2)}, u32[]{:S(2)}) collective-permute-start(f32[64,128]{1,0:T(8,128)S(1)} %get-tuple-element.15.own_ref), channel_id=1, source_target_pairs={{0,4},{8,12},{16,20},{24,28},{32,36},{40,44},{48,52},{56,60},{64,6... | collective-permute-start | bytes 98312 | tf_op jit(solution)/shard_map/ppermute | solution.py:39

commit v4 on v3

--- a/solution.py
+++ b/solution.py
@@ -12,16 +12,18 @@
 BF16 = jnp.bfloat16
 BESIDE = 1e9
 RUN = 4
+TURN = 2e10
 VMEM = pl.BlockSpec(memory_space=pltpu.VMEM)
 BLOCKS = pl.BlockSpec()
 
 
-def call(body, out, flops, traffic, *operands, spec=VMEM, limit=32):
+def call(body, out, flops, traffic, *operands, spec=VMEM, limit=32, scratch=()):
     return pl.pallas_call(
         body,
         out_shape=out,
         in_specs=[spec] * len(operands),
         out_specs=jax.tree.map(lambda _: VMEM, out),
+        scratch_shapes=scratch,
         cost_estimate=pl.CostEstimate(flops=int(flops), bytes_accessed=int(traffic), transcendentals=0),
         compiler_params=pltpu.CompilerParams(vmem_limit_bytes=limit * 1024 * 1024),
     )(*operands)
@@ -41,15 +43,20 @@
     return jnp.where(odd, swaps[1], swaps[0]), jnp.where(odd, swaps[0], swaps[1])
 
 
-def spread(x, axis):
-    count = lax.axis_size(axis)
-    inner, outer = x.shape[:2]
+def spread(x, axis, wide):
+    inner, room, outer, columns = x.shape
     runs = [[o * inner + i for i in range(inner)] for o in range(outer)]
     across = [[o * inner + i for o in range(outer)] for i in range(inner)]
     x = lax.all_to_all(x, axis, 0, 0, axis_index_groups=runs, tiled=True)
-    x = jnp.swapaxes(x, 0, 1)
-    x = lax.all_to_all(x, axis, 0, 0, axis_index_groups=across, tiled=True)
-    return x.reshape(count, *x.shape[2:])
+    x = call(
+        turn_body,
+        shape((outer, wide, columns), BF16),
+        TURN,
+        1e6,
+        x,
+        scratch=[pltpu.VMEM((outer * wide, columns), F32)],
+    )
+    return x, lax.all_to_all(x, axis, 0, 0, axis_index_groups=across, tiled=True)
 
 
 def split_two(x):
@@ -62,6 +69,36 @@
     rest = x - high.astype(F32)
     mid = rest.astype(BF16)
     return high, mid, (rest - mid.astype(F32)).astype(BF16)
+
+
+STEPS = 256
+LARGEST = 32600.0
+TAIL = 16
+
+
+def scale_of(steps):
+    return jnp.exp2(steps * (1.0 / STEPS))
+
+
+def encode(table, out_ref):
+    rows, columns = table.shape
+    most = jnp.max(jnp.abs(table), axis=0, keepdims=True)
+    steps = jnp.ceil(jnp.log2(jnp.maximum(most, 1e-30)) * STEPS)
+    coded = jnp.round(table * (LARGEST / scale_of(steps)))
+    out_ref[0:rows, :] = coded.astype(jnp.int32).astype(jnp.int16)
+    tail = jnp.broadcast_to(steps, (TAIL, columns))
+    out_ref[rows : rows + TAIL, :] = tail.astype(jnp.int32).astype(jnp.int16)
+
+
+def decode(parts_ref, low, high):
+    rows = parts_ref.shape[1] - TAIL
+    total = None
+    for k in range(parts_ref.shape[0]):
+        steps = parts_ref[k, rows : rows + TAIL, :].astype(jnp.int32).astype(F32)[0:1]
+        unit = scale_of(steps) * (1.0 / LARGEST)
+        part = parts_ref[k, low:high, :].astype(jnp.int32).astype(F32) * unit
+        total = part if total is None else total + part
+    return total
 
 
 WIDE = 12
@@ -149,7 +186,7 @@
     out_ref[...] = own_edges(n_ref[...], start, EDGE, lanes_of(packed.shape), packed)
 
 
-def message_body(fp_ref, counts_ref, rows_ref, values_ref, precision_ref, out_ref):
+def message_body(fp_ref, counts_ref, rows_ref, values_ref, precision_ref, out_ref, full_ref):
     cap, dests = rows_ref.shape
     slot = lax.broadcasted_iota(jnp.int32, (cap, dests), 0)
     live = slot < counts_ref[...]
@@ -160,19 +197,31 @@
     stacked = [x[c : c + 1] for c in range(cap) for x in items]
     stacked.append(jnp.zeros((out_ref.shape[3] - len(stacked), dests), F32))
     meta = jnp.concatenate(stacked, axis=0).T
-    place = lax.broadcasted_iota(jnp.int32, (dests, *out_ref.shape[2:]), 1)
     fp = fp_ref[...].astype(F32)
     fp = jnp.concatenate([fp, jnp.zeros_like(fp)], axis=1)
-    full = jnp.where(place == cap, meta[:, None, :], fp).astype(BF16)
-    inner, outer = out_ref.shape[:2]
-    full = full.reshape(outer, inner, *full.shape[1:])
+    stride = fp.shape[1]
+    place = lax.broadcasted_iota(jnp.int32, fp.shape, 1)
+    full_ref[...] = jnp.where(place == cap, meta[:, None, :], fp).reshape(full_ref.shape)
+    inner, room, outer = out_ref.shape[:3]
     for i in range(inner):
-        out_ref[i] = full[:, i]
-
-
-def first_body(fp_ref, counts_ref, rows_ref, values_ref, precision_ref, ens_ref, static_ref, e_ref, n_ref, out_ref, own_ref):
+        for r in range(room):
+            out_ref[i, r] = full_ref[pl.ds(stride * i + r, outer, stride=stride * inner), :].astype(BF16)
+
+
+def turn_body(in_ref, out_ref, rows_ref):
+    inner, room, outer, columns = in_ref.shape
+    wide = out_ref.shape[1]
+    for i in range(inner):
+        for r in range(room):
+            rows_ref[pl.ds(room * i + r, outer, stride=wide), :] = in_ref[i, r].astype(F32)
+    for r in range(inner * room, wide):
+        rows_ref[pl.ds(r, outer, stride=wide), :] = jnp.zeros((outer, columns), F32)
+    out_ref[...] = rows_ref[...].reshape(out_ref.shape).astype(BF16)
+
+
+def first_body(fp_ref, counts_ref, rows_ref, values_ref, precision_ref, ens_ref, static_ref, e_ref, n_ref, out_ref, own_ref, full_ref):
     edges_body(ens_ref, static_ref, e_ref, n_ref, own_ref)
-    message_body(fp_ref, counts_ref, rows_ref, values_ref, precision_ref, out_ref)
+    message_body(fp_ref, counts_ref, rows_ref, values_ref, precision_ref, out_ref, full_ref)
 
 
 def inner_increment_body(latitudes, scale, share, ens_ref, static_ref, sigma_ref, e_ref, n_ref, pert_ref, out_ref):
@@ -220,20 +269,18 @@
             total[t] = total[t] + pert_ref[m, t].astype(F32) * u
     static = (share * sigma_ref[...]) * place_edges(packed, members, lane)
     edge = at_edge(lane, columns)
+    table = []
     for t in range(slots):
-        span = slice(t * rows, (t + 1) * rows)
-        out_ref[span, :] = jnp.where(edge, scale * total[t] + static, inner_ref[span, :])
-
-
-def observe_body(cap, parts_ref, seen_ref, out_ref):
-    table = parts_ref[0]
-    for g in range(1, parts_ref.shape[0]):
-        table = table + parts_ref[g]
+        table.append(jnp.where(edge, scale * total[t] + static, inner_ref[t * rows : (t + 1) * rows, :]))
+    encode(jnp.concatenate(table, axis=0), out_ref)
+
+
+def observe_body(cap, wide, parts_ref, seen_ref, out_ref):
+    table = decode(parts_ref, 0, parts_ref.shape[1] - TAIL)
     rows, columns = table.shape
     high, low = split_two(table)
     seen = seen_ref[...]
     count = seen.shape[0]
-    room = seen.shape[0] // seen_ref.shape[0]
     group = 8
     eye_shape = (group * cap, columns)
     eye = (
@@ -243,7 +290,8 @@
     got = lax.dot_general(high, seen, contract, preferred_element_type=F32)
     got = got + lax.dot_general(low, seen, contract, preferred_element_type=F32)
     meta = lax.dot_general(eye, seen, contract, preferred_element_type=F32)
-    place = lax.broadcasted_iota(jnp.int32, (group, count), 1) & (group - 1)
+    at = lax.broadcasted_iota(jnp.int32, (group, count), 1) % wide
+    place = jnp.where(at < RUN * (cap + 1), at % (cap + 1), cap)
     facts = jnp.zeros((group, count), F32)
     for c in range(cap):
         part = pltpu.roll(meta[c * group : (c + 1) * group], count - (cap - c), 1)
@@ -259,18 +307,14 @@
         spread = jnp.where(hit, piece.astype(F32), 0.0).astype(BF16)
         term = jnp.dot(spread, seen, preferred_element_type=F32)
         out = term if out is None else out + term
-    out_ref[...] = out
+    encode(out, out_ref)
 
 
 def source_body(scale, parts_ref, pert_ref, sigma_ref, out_ref, packed_ref):
     members, slots, rows = pert_ref.shape[:3]
     gradient = []
     for t in range(slots):
-        span = slice(t * rows, (t + 1) * rows)
-        g = parts_ref[0, span, :]
-        for k in range(1, parts_ref.shape[0]):
-            g = g + parts_ref[k, span, :]
-        gradient.append(g)
+        gradient.append(decode(parts_ref, t * rows, (t + 1) * rows))
     fields = []
     for m in range(members):
         u = pert_ref[m, 0].astype(F32) * gradient[0]
@@ -337,10 +381,11 @@
 
     field = shape((rows, columns))
 
-    room = 8
+    room = cap + 1
+    wide = -(-RUN * room // 8) * 8
     message, own = call(
         first_body,
-        (shape((RUN, tiles // RUN, room, columns), BF16), field),
+        (shape((RUN, room, tiles // RUN, columns), BF16), field),
         1e6,
         1e6,
         footprints[0, 0],
@@ -354,18 +399,21 @@
         n,
         spec=BLOCKS,
         limit=60,
+        scratch=[pltpu.VMEM((tiles * 2 * cap, columns), F32)],
     )
     west, east = from_neighbours(own, "tile")
-    seen = spread(message, "tile")
+    turned, seen = spread(message, "tile", wide)
+    late, _ = lax.optimization_barrier((static, turned))
 
     share = 1.0 / groups
+    coded = shape((table_rows + TAIL, columns), jnp.int16)
     inner = call(
         lambda *refs: inner_increment_body(latitudes, scale, share, *refs),
         shape((table_rows, columns)),
         BESIDE,
         4e6,
         ens,
-        static,
+        late,
         sigma,
         e,
         n,
@@ -373,7 +421,7 @@
     )
     partial, e_packed, n_packed = call(
         lambda *refs: outer_increment_body(latitudes, scale, share, *refs),
-        (shape((table_rows, columns)), field, field),
+        (coded, field, field),
         1e7,
         4e6,
         inner,
@@ -387,12 +435,12 @@
     )
     parts = lax.all_gather(partial, "mem")
     partial_grad = call(
-        lambda *refs: observe_body(cap, *refs),
-        shape((table_rows, columns)),
+        lambda *refs: observe_body(cap, wide, *refs),
+        coded,
         3e8,
         4e6,
         parts,
-        seen.reshape(tiles * room, columns),
+        seen.reshape(-1, columns),
     )
     grad_parts = lax.all_gather(partial_grad, "mem")
     source, own_source = call(

time: 67.6 us -> 65.6 us (0.970)
  blocking collectives: 20.6 us -> 18.6 us
  starting transfers between devices: 35.8 us -> 33.8 us
  waiting for transfers between devices: 2.48 us -> 4.23 us
  Pallas kernels: 6.64 us -> 7.51 us
  local copies, waits for them, and re-layouts: 0.78 us -> 0.04 us
    all_gather x1, blocking collectives: 12.7 us -> 9.91 us  [on_device(): parts = lax.all_gather(partial, 'mem')]
    ppermute x4, starting transfers between devices: 26.4 us -> 24.4 us  [from_neighbours(): swaps.append(lax.ppermute(x, axis, pairs + [(j, i) for i, j in pairs]))]
    ppermute x4, waiting for transfers between devices: 2.48 us -> 4.18 us  [from_neighbours(): swaps.append(lax.ppermute(x, axis, pairs + [(j, i) for i, j in pairs]))]
    pallas_call x7 -> x8, Pallas kernels: 6.64 us -> 7.51 us  [call(): pl.pallas_call(body, out_shape=out, in_specs=[spec] * len(operands), out_...]
    all_gather x1, blocking collectives: 7.9 us -> 8.73 us  [on_device(): grad_parts = lax.all_gather(partial_grad, 'mem')]
    transpose x1 -> x0, local copies, waits for them, and re-layouts: 0.75 us -> none  [spread(): x = jnp.swapaxes(x, 0, 1)]
  transfers between devices with their start and end apart: 6 -> 6, of which waited for: 2 -> 1; matrix products, arithmetic and copies ran while one was open for 1% -> 0% of each run, Pallas kernels for 3% -> 4%
where the time goes in v4:
time: 65.6 us; the launch traced here: 65.1 us
  starting transfers between devices  33.8 us (52%)
  blocking collectives  18.6 us (28%)
  Pallas kernels  7.51 us (11%)
  waiting for transfers between devices  4.23 us (6%)
  between operations  0.85 us (1%)
    ppermute x4, starting transfers between devices, from_neighbours(): swaps.append(lax.ppermute(x, axis, pairs + [(j, i) for i, j in pairs]))  24.4 us
    all_gather x1, blocking collectives, on_device(): parts = lax.all_gather(partial, 'mem')  9.91 us
    all_gather x1, blocking collectives, on_device(): grad_parts = lax.all_gather(partial_grad, 'mem')  8.73 us
    pallas_call x8, Pallas kernels, call(): pl.pallas_call(body, out_shape=out, in_specs=[spec] * len(operands), out_...  7.51 us
    all_to_all x1, starting transfers between devices, spread(): x = lax.all_to_all(x, axis, 0, 0, axis_index_groups=runs, tiled=True)  4.97 us
    all_to_all x1, starting transfers between devices, spread(): lax.all_to_all(x, axis, 0, 0, axis_index_groups=across, tiled=True)  4.44 us
    ppermute x4, waiting for transfers between devices, from_neighbours(): swaps.append(lax.ppermute(x, axis, pairs + [(j, i) for i, j in pairs]))  4.18 us
  transfers between devices with their start and end apart: 6, of which 1 were waited for; matrix products, arithmetic and copies ran while one was open for 0% of the time, Pallas kernels for 4%

profile of v4, /device:TPU:1, one launch (start us, length us, event | category | flops | bytes accessed | tf_op | source)
XLA Modules:
  0.0 65.1 jit_solution(1198903739376856271)
XLA Ops:
  0.6 2.2 %shard_map.122 = (bf16[4,5,32,128]{3,2,1,0:T(8,128)(2,1)}, f32[64,128]{1,0:T(8,128)}) custom-call(bf16[128,4,128]{2,1,0:T(4,128)(2,1)} %bitcast.45, s32[1,128]{1,0:T(1,128)} %bitcast.49, s32[4,128]{1,0:T(4,128)} %bitcast.46, f32[4,128]{1,0:T(4,128)} %bitcast.47, f32[4,128]{1,0:T(4,128)} %bitcast.48, f32[8,64,128]{2,1,0:T(8,128)} %bitcast.27, ...), custom_call_target="tpu_custom_call" | custom-call | flops 1000000 | bytes 1000000 | tf_op jit(solution)/shard_map/pallas_call | solution.py:21
  2.8 5.0 %all-to-all-start = ((bf16[4,5,32,128]{3,2,1,0:T(8,128)(2,1)}), bf16[4,5,32,128]{3,2,1,0:T(8,128)(2,1)S(1)}, u32[]{:S(2)}, u32[]{:S(2)}) async-start(bf16[4,5,32,128]{3,2,1,0:T(8,128)(2,1)} %get-tuple-element.12), calls=%async_computation | async-start | bytes 327680 | tf_op jit(solution)/shard_map/all_to_all | solution.py:50
  7.8 15.9 %collective-permute-start.1 = (f32[64,128]{1,0:T(8,128)S(1)}, f32[64,128]{1,0:T(8,128)S(1)}, u32[]{:S(2)}, u32[]{:S(2)}) collective-permute-start(f32[64,128]{1,0:T(8,128)S(1)} %copy-done.5), channel_id=1, source_target_pairs={{4,8},{12,16},{20,24},{28,32},{36,40},{44,48},{52,56},{60,64},{68,... | collective-permute-start | bytes 98312 | tf_op jit(solution)/shard_map/ppermute | solution.py:41
  23.7 1.9 %collective-permute-start = (f32[64,128]{1,0:T(8,128)S(1)}, f32[64,128]{1,0:T(8,128)S(1)}, u32[]{:S(2)}, u32[]{:S(2)}) collective-permute-start(f32[64,128]{1,0:T(8,128)S(1)} %copy-done.5), channel_id=1, source_target_pairs={{0,4},{8,12},{16,20},{24,28},{32,36},{40,44},{48,52},{56,60},{64,6... | collective-permute-start | bytes 98312 | tf_op jit(solution)/shard_map/ppermute | solution.py:41
  25.7 0.0 all-to-all-done.in_ref
  25.7 0.0 copy-start.1
  25.7 0.0 copy-start.2
  25.7 0.0 copy-start.3
  25.7 0.0 copy-start.4
  25.7 0.0 copy-start.6
  25.7 0.8 %shard_map.123 = bf16[32,24,128]{2,1,0:T(8,128)(2,1)} custom-call(bf16[4,5,32,128]{3,2,1,0:T(8,128)(2,1)S(1)} %all-to-all-done.in_ref), custom_call_target="tpu_custom_call" | custom-call | flops 20000000000 | bytes 1000000 | tf_op jit(solution)/shard_map/pallas_call | solution.py:21
  26.5 4.4 %all-to-all-start.1 = ((bf16[32,24,128]{2,1,0:T(8,128)(2,1)}), bf16[32,24,128]{2,1,0:T(8,128)(2,1)S(1)}, u32[]{:S(2)}, u32[]{:S(2)}) async-start(bf16[32,24,128]{2,1,0:T(8,128)(2,1)} %shard_map.123), calls=%async_computation.1 | async-start | bytes 393216 | tf_op jit(solution)/shard_map/all_to_all | solution.py:59
  31.0 0.6 shard_map.124.refs_0_
  31.6 0.9 %shard_map.125 = (s16[272,128]{1,0:T(8,128)(2,1)S(1)}, f32[64,128]{1,0:T(8,128)S(1)}, f32[64,128]{1,0:T(8,128)S(1)}) custom-call(f32[256,128]{1,0:T(8,128)S(1)} %shard_map.124.refs_0_, f32[64,128]{1,0:T(8,128)S(1)} %copy-done.5, f32[64,128]{1,0:T(8,128)S(1)} %get-tuple-element.25.refs_2_, f32[64,128]{1,0:T(8,128)S(1)} %get-tuple-element.24.refs_3_, ...), custom_call_target="tpu_custom_call" | custom-call | flops 10000000 | bytes 4000000 | tf_op jit(solution)/shard_map/pallas_call | solution.py:21
  32.5 9.9 %all-gather = s16[1088,128]{1,0:T(8,128)(2,1)S(1)} all-gather(s16[272,128]{1,0:T(8,128)(2,1)S(1)} %get-tuple-element.15), channel_id=2, replica_groups=mesh['tile'=128,'mem'=4] {'mem'}, dimensions={0}, use_global_device_ids=true | all-gather | bytes 348160 | tf_op jit(solution)/shard_map/all_gather | solution.py:436
  42.5 0.0 all-to-all-done.1
  42.5 1.0 %shard_map.126 = s16[272,128]{1,0:T(8,128)(2,1)S(1)} custom-call(s16[4,272,128]{2,1,0:T(8,128)(2,1)S(1)} %bitcast.26, bf16[768,128]{1,0:T(8,128)(2,1)S(1)} %bitcast.30), custom_call_target="tpu_custom_call" | custom-call | flops 300000000 | bytes 4000000 | tf_op jit(solution)/shard_map/pallas_call | solution.py:21
  43.5 8.7 %all-gather.1 = s16[1088,128]{1,0:T(8,128)(2,1)S(1)} all-gather(s16[272,128]{1,0:T(8,128)(2,1)S(1)} %shard_map.126), channel_id=3, replica_groups=mesh['tile'=128,'mem'=4] {'mem'}, dimensions={0}, use_global_device_ids=true | all-gather | bytes 348160 | tf_op jit(solution)/shard_map/all_gather | solution.py:445
  52.2 0.3 shard_map.127
  52.5 4.6 %collective-permute-start.3 = (f32[64,128]{1,0:T(8,128)S(1)}, f32[64,128]{1,0:T(8,128)S(1)}, u32[]{:S(2)}, u32[]{:S(2)}) collective-permute-start(f32[64,128]{1,0:T(8,128)S(1)} %get-tuple-element.17.own_ref), channel_id=1, source_target_pairs={{4,8},{12,16},{20,24},{28,32},{36,40},{44,48},{52,56},{60,64},{68,... | collective-permute-start | bytes 98312 | tf_op jit(solution)/shard_map/ppermute | solution.py:41
  57.2 1.9 %collective-permute-start.2 = (f32[64,128]{1,0:T(8,128)S(1)}, f32[64,128]{1,0:T(8,128)S(1)}, u32[]{:S(2)}, u32[]{:S(2)}) collective-permute-start(f32[64,128]{1,0:T(8,128)S(1)} %get-tuple-element.17.own_ref), channel_id=1, source_target_pairs={{0,4},{8,12},{16,20},{24,28},{32,36},{40,44},{48,52},{56,60},{64,6... | collective-permute-start | bytes 98312 | tf_op jit(solution)/shard_map/ppermute | solution.py:41
  59.1 0.5 shard_map.128.inner_ref
  59.7 4.2 %collective-permute-done.3 = f32[64,128]{1,0:T(8,128)S(1)} collective-permute-done((f32[64,128]{1,0:T(8,128)S(1)}, f32[64,128]{1,0:T(8,128)S(1)}, u32[]{:S(2)}, u32[]{:S(2)}) %collective-permute-start.3) | collective-permute-done | bytes 32800 | tf_op jit(solution)/shard_map/ppermute | solution.py:41
  63.9 1.3 %shard_map.129 = (f32[8,64,128]{2,1,0:T(8,128)}, f32[64,128]{1,0:T(8,128)}) custom-call(f32[9,64,128]{2,1,0:T(8,128)S(1)} %shard_map.128.inner_ref, f32[64,128]{1,0:T(8,128)S(1)} %get-tuple-element.17.own_ref, f32[64,128]{1,0:T(8,128)S(1)} %get-tuple-element.23.west_ref, f32[64,128]{1,0:T(8,128)S(1)} %get-tuple-element.22.east_ref, f32[64,128]{1,0:T(8,128)S(1)} %copy-done.5, ...), custom_call_target="tpu_custom_call" | custom-call | flops 10000000 | bytes 2000000 | tf_op jit(solution)/shard_map/pallas_call | solution.py:21
  (14 shorter events, 0.0 us)
Async XLA Ops:
  2.8 5.0 %copy-start.5 = (f32[64,128]{1,0:T(8,128)S(1)}, f32[64,128]{1,0:T(8,128)}, u32[]{:S(2)}) copy-start(f32[64,128]{1,0:T(8,128)} %get-tuple-element.14.refs_1_.controls_ref) | copy-start | bytes 98308
  2.8 22.9 %all-to-all-start = ((bf16[4,5,32,128]{3,2,1,0:T(8,128)(2,1)}), bf16[4,5,32,128]{3,2,1,0:T(8,128)(2,1)S(1)}, u32[]{:S(2)}, u32[]{:S(2)}) async-start(bf16[4,5,32,128]{3,2,1,0:T(8,128)(2,1)} %get-tuple-element.12), calls=%async_computation | async-start | bytes 327680 | tf_op jit(solution)/shard_map/all_to_all | solution.py:50
  7.8 23.2 %collective-permute-start.1 = (f32[64,128]{1,0:T(8,128)S(1)}, f32[64,128]{1,0:T(8,128)S(1)}, u32[]{:S(2)}, u32[]{:S(2)}) collective-permute-start(f32[64,128]{1,0:T(8,128)S(1)} %copy-done.5), channel_id=1, source_target_pairs={{4,8},{12,16},{20,24},{28,32},{36,40},{44,48},{52,56},{60,64},{68,... | collective-permute-start | bytes 98312 | tf_op jit(solution)/shard_map/ppermute | solution.py:41
  23.7 7.2 %collective-permute-start = (f32[64,128]{1,0:T(8,128)S(1)}, f32[64,128]{1,0:T(8,128)S(1)}, u32[]{:S(2)}, u32[]{:S(2)}) collective-permute-start(f32[64,128]{1,0:T(8,128)S(1)} %copy-done.5), channel_id=1, source_target_pairs={{0,4},{8,12},{16,20},{24,28},{32,36},{40,44},{48,52},{56,60},{64,6... | collective-permute-start | bytes 98312 | tf_op jit(solution)/shard_map/ppermute | solution.py:41
  25.7 5.3 %copy-start.1 = (f32[8,2,32,128]{3,2,1,0:T(8,128)S(1)}, f32[8,2,32,128]{3,2,1,0:T(8,128)}, u32[]{:S(2)}) copy-start(f32[8,2,32,128]{3,2,1,0:T(8,128)} %param.11) | copy-start | bytes 786436
  25.7 5.3 %copy-start.2 = (f32[2,32,128]{2,1,0:T(8,128)S(1)}, f32[2,32,128]{2,1,0:T(8,128)}, u32[]{:S(2)}) copy-start(f32[2,32,128]{2,1,0:T(8,128)} %param.13) | copy-start | bytes 98308
  25.7 5.3 %copy-start.3 = (f32[2,32,128]{2,1,0:T(8,128)S(1)}, f32[2,32,128]{2,1,0:T(8,128)}, u32[]{:S(2)}) copy-start(f32[2,32,128]{2,1,0:T(8,128)} %param.14) | copy-start | bytes 98308
  25.7 5.3 %copy-start.4 = (f32[2,32,128]{2,1,0:T(8,128)S(1)}, f32[2,32,128]{2,1,0:T(8,128)}, u32[]{:S(2)}) copy-start(f32[2,32,128]{2,1,0:T(8,128)} %param.15) | copy-start | bytes 98308
  25.7 5.3 %copy-start.6 = (f32[2,32,128]{2,1,0:T(8,128)S(1)}, f32[2,32,128]{2,1,0:T(8,128)}, u32[]{:S(2)}) copy-start(f32[2,32,128]{2,1,0:T(8,128)} %param.12) | copy-start | bytes 98308
  26.5 4.5 %copy-start = (bf16[8,4,2,32,128]{4,3,2,1,0:T(8,128)(2,1)S(1)}, bf16[8,4,2,32,128]{4,3,2,1,0:T(8,128)(2,1)}, u32[]{:S(2)}) copy-start(bf16[8,4,2,32,128]{4,3,2,1,0:T(8,128)(2,1)} %param.16) | copy-start | bytes 1572868
  26.5 16.0 %all-to-all-start.1 = ((bf16[32,24,128]{2,1,0:T(8,128)(2,1)}), bf16[32,24,128]{2,1,0:T(8,128)(2,1)S(1)}, u32[]{:S(2)}, u32[]{:S(2)}) async-start(bf16[32,24,128]{2,1,0:T(8,128)(2,1)} %shard_map.123), calls=%async_computation.1 | async-start | bytes 393216 | tf_op jit(solution)/shard_map/all_to_all | solution.py:59
  52.5 11.3 %collective-permute-start.3 = (f32[64,128]{1,0:T(8,128)S(1)}, f32[64,128]{1,0:T(8,128)S(1)}, u32[]{:S(2)}, u32[]{:S(2)}) collective-permute-start(f32[64,128]{1,0:T(8,128)S(1)} %get-tuple-element.17.own_ref), channel_id=1, source_target_pairs={{4,8},{12,16},{20,24},{28,32},{36,40},{44,48},{52,56},{60,64},{68,... | collective-permute-start | bytes 98312 | tf_op jit(solution)/shard_map/ppermute | solution.py:41
  57.2 6.7 %collective-permute-start.2 = (f32[64,128]{1,0:T(8,128)S(1)}, f32[64,128]{1,0:T(8,128)S(1)}, u32[]{:S(2)}, u32[]{:S(2)}) collective-permute-start(f32[64,128]{1,0:T(8,128)S(1)} %get-tuple-element.17.own_ref), channel_id=1, source_target_pairs={{0,4},{8,12},{16,20},{24,28},{32,36},{40,44},{48,52},{56,60},{64,6... | collective-permute-start | bytes 98312 | tf_op jit(solution)/shard_map/ppermute | solution.py:41

commit v5 on v4

--- a/solution.py
+++ b/solution.py
@@ -1,3 +1,4 @@
+import functools
 import math
 
 import jax
@@ -14,14 +15,15 @@
 RUN = 4
 TURN = 2e10
 VMEM = pl.BlockSpec(memory_space=pltpu.VMEM)
+SCALAR = pl.BlockSpec(memory_space=pltpu.SMEM)
 BLOCKS = pl.BlockSpec()
 
 
-def call(body, out, flops, traffic, *operands, spec=VMEM, limit=32, scratch=()):
+def call(body, out, flops, traffic, *operands, spec=VMEM, specs=None, limit=32, scratch=()):
     return pl.pallas_call(
         body,
         out_shape=out,
-        in_specs=[spec] * len(operands),
+        in_specs=specs or [spec] * len(operands),
         out_specs=jax.tree.map(lambda _: VMEM, out),
         scratch_shapes=scratch,
         cost_estimate=pl.CostEstimate(flops=int(flops), bytes_accessed=int(traffic), transcendentals=0),
@@ -43,20 +45,16 @@
     return jnp.where(odd, swaps[1], swaps[0]), jnp.where(odd, swaps[0], swaps[1])
 
 
-def spread(x, axis, wide):
-    inner, room, outer, columns = x.shape
-    runs = [[o * inner + i for i in range(inner)] for o in range(outer)]
-    across = [[o * inner + i for o in range(outer)] for i in range(inner)]
-    x = lax.all_to_all(x, axis, 0, 0, axis_index_groups=runs, tiled=True)
-    x = call(
-        turn_body,
-        shape((outer, wide, columns), BF16),
-        TURN,
-        1e6,
-        x,
-        scratch=[pltpu.VMEM((outer * wide, columns), F32)],
-    )
-    return x, lax.all_to_all(x, axis, 0, 0, axis_index_groups=across, tiled=True)
+def runs_of(axis):
+    outer = lax.axis_size(axis) // RUN
+    runs = [[o * RUN + i for i in range(RUN)] for o in range(outer)]
+    return runs, [list(tiles) for tiles in zip(*runs)]
+
+
+def between_runs(x, axis):
+    count = lax.axis_size(axis)
+    pairs = [((i + RUN - 1) % count, (i + RUN) % count) for i in range(0, count, RUN)]
+    return lax.ppermute(x, axis, pairs + [(j, i) for i, j in pairs])
 
 
 def split_two(x):
@@ -195,33 +193,49 @@
     items += [x.astype(F32) for x in split_three(jnp.where(live, precision_ref[...], 0.0))]
     items += [jnp.zeros((cap, dests), F32)]
     stacked = [x[c : c + 1] for c in range(cap) for x in items]
-    stacked.append(jnp.zeros((out_ref.shape[3] - len(stacked), dests), F32))
+    stacked.append(jnp.zeros((out_ref.shape[2] - len(stacked), dests), F32))
     meta = jnp.concatenate(stacked, axis=0).T
     fp = fp_ref[...].astype(F32)
     fp = jnp.concatenate([fp, jnp.zeros_like(fp)], axis=1)
     stride = fp.shape[1]
     place = lax.broadcasted_iota(jnp.int32, fp.shape, 1)
     full_ref[...] = jnp.where(place == cap, meta[:, None, :], fp).reshape(full_ref.shape)
-    inner, room, outer = out_ref.shape[:3]
+    inner = out_ref.shape[0]
+    outer = dests // inner
+    for i in range(inner):
+        for r in range(cap + 1):
+            part = full_ref[pl.ds(stride * i + r, outer, stride=stride * inner), :]
+            out_ref[i, r * outer : (r + 1) * outer, :] = part.astype(BF16)
+
+
+def turn_body(room, x_ref, in_ref, out_ref, west_ref, east_ref, rows_ref):
+    inner, columns = in_ref.shape[0], in_ref.shape[2]
+    outer, wide = out_ref.shape[:2]
     for i in range(inner):
         for r in range(room):
-            out_ref[i, r] = full_ref[pl.ds(stride * i + r, outer, stride=stride * inner), :].astype(BF16)
-
-
-def turn_body(in_ref, out_ref, rows_ref):
-    inner, room, outer, columns = in_ref.shape
-    wide = out_ref.shape[1]
-    for i in range(inner):
-        for r in range(room):
-            rows_ref[pl.ds(room * i + r, outer, stride=wide), :] = in_ref[i, r].astype(F32)
+            part = in_ref[i, r * outer : (r + 1) * outer, :].astype(F32)
+            rows_ref[pl.ds(room * i + r, outer, stride=wide), :] = part
     for r in range(inner * room, wide):
         rows_ref[pl.ds(r, outer, stride=wide), :] = jnp.zeros((outer, columns), F32)
     out_ref[...] = rows_ref[...].reshape(out_ref.shape).astype(BF16)
+    rows = west_ref.shape[0]
+    high = room * outer
+    x = x_ref[0]
+    for at, ref in ((x - 1, west_ref), (x + 1, east_ref)):
+        at = jnp.clip(at, 0, inner - 1)
+        edges = in_ref[at, high : high + rows, :].astype(F32)
+        ref[...] = edges + in_ref[at, high + rows : high + 2 * rows, :].astype(F32)
 
 
 def first_body(fp_ref, counts_ref, rows_ref, values_ref, precision_ref, ens_ref, static_ref, e_ref, n_ref, out_ref, own_ref, full_ref):
     edges_body(ens_ref, static_ref, e_ref, n_ref, own_ref)
     message_body(fp_ref, counts_ref, rows_ref, values_ref, precision_ref, out_ref, full_ref)
+    rows = own_ref.shape[0]
+    at = out_ref.shape[1] - 2 * rows
+    for piece in split_two(own_ref[...]):
+        for i in range(out_ref.shape[0]):
+            out_ref[i, at : at + rows, :] = piece
+        at += rows
 
 
 def inner_increment_body(latitudes, scale, share, ens_ref, static_ref, sigma_ref, e_ref, n_ref, pert_ref, out_ref):
@@ -240,13 +254,15 @@
 
 
 def outer_increment_body(
-    latitudes, scale, share, inner_ref, own_ref, west_ref, east_ref, sigma_ref, e_ref, n_ref, pert_ref, out_ref, e_out, n_out
+    latitudes, scale, share, x_ref, inner_ref, own_ref, far_ref, west_ref, east_ref, sigma_ref, e_ref, n_ref, pert_ref, out_ref, e_out, n_out
 ):
     members, slots = pert_ref.shape[:2]
     rows, columns = e_ref.shape
     fields = members + 1
     lane = lanes_of(e_ref.shape)
-    own, from_west, from_east = own_ref[...], west_ref[...], east_ref[...]
+    own, far, x = own_ref[...], far_ref[...], x_ref[0]
+    from_west = jnp.where(x == 0, far, west_ref[...])
+    from_east = jnp.where(x == RUN - 1, far, east_ref[...])
 
     def coefficient(x, west, west_at, east, east_at):
         first = own_edges(x, EDGE, WIDE // 2 - EDGE, lane, jnp.zeros(x.shape, F32))
@@ -383,9 +399,11 @@
 
     room = cap + 1
     wide = -(-RUN * room // 8) * 8
+    runs, across = runs_of("tile")
+    outer = len(runs)
     message, own = call(
         first_body,
-        (shape((RUN, room, tiles // RUN, columns), BF16), field),
+        (shape((RUN, room * outer + 2 * rows, columns), BF16), field),
         1e6,
         1e6,
         footprints[0, 0],
@@ -401,9 +419,21 @@
         limit=60,
         scratch=[pltpu.VMEM((tiles * 2 * cap, columns), F32)],
     )
-    west, east = from_neighbours(own, "tile")
-    turned, seen = spread(message, "tile", wide)
-    late, _ = lax.optimization_barrier((static, turned))
+    message = lax.all_to_all(message, "tile", 0, 0, axis_index_groups=runs, tiled=True)
+    far = between_runs(own, "tile")
+    x = (lax.axis_index("tile") % RUN).reshape(1)
+    message, west, east = call(
+        functools.partial(turn_body, room),
+        (shape((outer, wide, columns), BF16), field, field),
+        TURN,
+        1e6,
+        x,
+        message,
+        specs=[SCALAR, VMEM],
+        scratch=[pltpu.VMEM((outer * wide, columns), F32)],
+    )
+    seen = lax.all_to_all(message, "tile", 0, 0, axis_index_groups=across, tiled=True)
+    late, _ = lax.optimization_barrier((static, message))
 
     share = 1.0 / groups
     coded = shape((table_rows + TAIL, columns), jnp.int16)
@@ -422,16 +452,19 @@
     partial, e_packed, n_packed = call(
         lambda *refs: outer_increment_body(latitudes, scale, share, *refs),
         (coded, field, field),
-        1e7,
+        4e9,
         4e6,
+        x,
         inner,
         own,
+        far,
         west,
         east,
         sigma,
         e,
         n,
         pert,
+        specs=[SCALAR] + [VMEM] * 9,
     )
     parts = lax.all_gather(partial, "mem")
     partial_grad = call(

time: 65.6 us -> 65.4 us (level)
  starting transfers between devices: 33.8 us -> 32.6 us
    ppermute x4 -> x2, starting transfers between devices: 24.4 us -> 6.04 us  [from_neighbours(): swaps.append(lax.ppermute(x, axis, pairs + [(j, i) for i, j in pairs]))]
    ppermute x0 -> x1, starting transfers between devices: none -> 15.9 us  [between_runs(): return lax.ppermute(x, axis, pairs + [(j, i) for i, j in pairs])]
    all_to_all x2, starting transfers between devices: 9.41 us -> 10.6 us  [the longest x1 5.64 us: on_device(): lax.all_to_all(message, 'tile', 0, 0, axis_index_groups=across, tiled=True)]
    ppermute x4 -> x2, waiting for transfers between devices: 4.18 us -> 4.71 us  [from_neighbours(): swaps.append(lax.ppermute(x, axis, pairs + [(j, i) for i, j in pairs]))]
  transfers between devices with their start and end apart: 6 -> 5, of which waited for: 1 -> 2; matrix products, arithmetic and copies ran while one was open for 0% -> 0% of each run, Pallas kernels for 4% -> 4%
where the time goes in v5:
time: 65.4 us; the launch traced here: 64.9 us
  starting transfers between devices  32.6 us (50%)
  blocking collectives  19 us (29%)
  Pallas kernels  7.63 us (12%)
  waiting for transfers between devices  4.88 us (7%)
  between operations  0.81 us (1%)
    ppermute x1, starting transfers between devices, between_runs(): return lax.ppermute(x, axis, pairs + [(j, i) for i, j in pairs])  15.9 us
    all_gather x1, blocking collectives, on_device(): parts = lax.all_gather(partial, 'mem')  9.88 us
    all_gather x1, blocking collectives, on_device(): grad_parts = lax.all_gather(partial_grad, 'mem')  9.1 us
    pallas_call x8, Pallas kernels, call(): pl.pallas_call(body, out_shape=out, in_specs=specs or [spec] * len(operan...  7.63 us
    ppermute x2, starting transfers between devices, from_neighbours(): swaps.append(lax.ppermute(x, axis, pairs + [(j, i) for i, j in pairs]))  6.04 us
    all_to_all x1, starting transfers between devices, on_device(): lax.all_to_all(message, 'tile', 0, 0, axis_index_groups=across, tiled=True)  5.64 us
    all_to_all x1, starting transfers between devices, on_device(): lax.all_to_all(message, 'tile', 0, 0, axis_index_groups=runs, tiled=True)  4.97 us
    ppermute x2, waiting for transfers between devices, from_neighbours(): swaps.append(lax.ppermute(x, axis, pairs + [(j, i) for i, j in pairs]))  4.71 us
  transfers between devices with their start and end apart: 5, of which 2 were waited for; matrix products, arithmetic and copies ran while one was open for 0% of the time, Pallas kernels for 4%

profile of v5, /device:TPU:1, one launch (start us, length us, event | category | flops | bytes accessed | tf_op | source)
XLA Modules:
  0.0 64.9 jit_solution(5506124917025497563)
XLA Ops:
  0.6 2.3 %shard_map.122 = (bf16[4,288,128]{2,1,0:T(8,128)(2,1)}, f32[64,128]{1,0:T(8,128)}) custom-call(bf16[128,4,128]{2,1,0:T(4,128)(2,1)} %bitcast.46, s32[1,128]{1,0:T(1,128)} %bitcast.50, s32[4,128]{1,0:T(4,128)} %bitcast.47, f32[4,128]{1,0:T(4,128)} %bitcast.48, f32[4,128]{1,0:T(4,128)} %bitcast.49, f32[8,64,128]{2,1,0:T(8,128)} %bitcast.28, ...), custom_call_target="tpu_custom_call" | custom-call | flops 1000000 | bytes 1000000 | tf_op jit(solution)/shard_map/pallas_call | solution.py:23
  2.9 5.0 %all-to-all-start = ((bf16[4,288,128]{2,1,0:T(8,128)(2,1)}), bf16[4,288,128]{2,1,0:T(8,128)(2,1)S(1)}, u32[]{:S(2)}, u32[]{:S(2)}) async-start(bf16[4,288,128]{2,1,0:T(8,128)(2,1)} %get-tuple-element.15), calls=%async_computation | async-start | bytes 589824 | tf_op jit(solution)/shard_map/all_to_all | solution.py:422
  7.9 0.0 copy-done.6
  7.9 15.9 %collective-permute-start = (f32[64,128]{1,0:T(8,128)S(1)}, f32[64,128]{1,0:T(8,128)S(1)}, u32[]{:S(2)}, u32[]{:S(2)}) collective-permute-start(f32[64,128]{1,0:T(8,128)S(1)} %copy-done.6), channel_id=1, source_target_pairs={{12,16},{28,32},{44,48},{60,64},{76,80},{92,96},{108,112},{124,128... | collective-permute-start | bytes 98312 | tf_op jit(solution)/shard_map/ppermute | solution.py:57
  23.8 0.0 all-to-all-done.in_ref
  23.9 0.0 copy-start
  23.9 0.8 %shard_map.123 = (bf16[32,24,128]{2,1,0:T(8,128)(2,1)}, f32[64,128]{1,0:T(8,128)S(1)}, f32[64,128]{1,0:T(8,128)S(1)}) custom-call(s32[1]{0:T(128)} %bitcast.x_ref.refs_0_, bf16[4,288,128]{2,1,0:T(8,128)(2,1)S(1)} %all-to-all-done.in_ref), custom_call_target="tpu_custom_call" | custom-call | flops 20000000000 | bytes 1000000 | tf_op jit(solution)/shard_map/pallas_call | solution.py:23
  24.6 0.0 copy-start.5
  24.7 5.6 %all-to-all-start.1 = ((bf16[32,24,128]{2,1,0:T(8,128)(2,1)}), bf16[32,24,128]{2,1,0:T(8,128)(2,1)S(1)}, u32[]{:S(2)}, u32[]{:S(2)}) async-start(bf16[32,24,128]{2,1,0:T(8,128)(2,1)} %get-tuple-element.16), calls=%async_computation.1 | async-start | bytes 393216 | tf_op jit(solution)/shard_map/all_to_all | solution.py:435
  30.3 0.0 copy-done
  30.4 0.6 shard_map.124.refs_1_
  31.0 0.0 collective-permute-done.refs_3_
  31.0 0.9 %shard_map.125 = (s16[272,128]{1,0:T(8,128)(2,1)S(1)}, f32[64,128]{1,0:T(8,128)S(1)}, f32[64,128]{1,0:T(8,128)S(1)}) custom-call(s32[1]{0:T(128)} %bitcast.x_ref.refs_0_, f32[256,128]{1,0:T(8,128)S(1)} %shard_map.124.refs_1_, f32[64,128]{1,0:T(8,128)S(1)} %copy-done.6, f32[64,128]{1,0:T(8,128)S(1)} %collective-permute-done.refs_3_, ...), custom_call_target="tpu_custom_call" | custom-call | flops 4000000000 | bytes 4000000 | tf_op jit(solution)/shard_map/pallas_call | solution.py:23
  31.9 9.9 %all-gather = s16[1088,128]{1,0:T(8,128)(2,1)S(1)} all-gather(s16[272,128]{1,0:T(8,128)(2,1)S(1)} %get-tuple-element.21), channel_id=2, replica_groups=mesh['tile'=128,'mem'=4] {'mem'}, dimensions={0}, use_global_device_ids=true | all-gather | bytes 348160 | tf_op jit(solution)/shard_map/all_gather | solution.py:469
  41.8 0.2 all-to-all-done.1
  41.9 1.0 %shard_map.126 = s16[272,128]{1,0:T(8,128)(2,1)S(1)} custom-call(s16[4,272,128]{2,1,0:T(8,128)(2,1)S(1)} %bitcast.27, bf16[768,128]{1,0:T(8,128)(2,1)S(1)} %bitcast.31), custom_call_target="tpu_custom_call" | custom-call | flops 300000000 | bytes 4000000 | tf_op jit(solution)/shard_map/pallas_call | solution.py:23
  42.9 9.1 %all-gather.1 = s16[1088,128]{1,0:T(8,128)(2,1)S(1)} all-gather(s16[272,128]{1,0:T(8,128)(2,1)S(1)} %shard_map.126), channel_id=3, replica_groups=mesh['tile'=128,'mem'=4] {'mem'}, dimensions={0}, use_global_device_ids=true | all-gather | bytes 348160 | tf_op jit(solution)/shard_map/all_gather | solution.py:478
  52.0 0.3 shard_map.127
  52.3 4.1 %collective-permute-start.2 = (f32[64,128]{1,0:T(8,128)S(1)}, f32[64,128]{1,0:T(8,128)S(1)}, u32[]{:S(2)}, u32[]{:S(2)}) collective-permute-start(f32[64,128]{1,0:T(8,128)S(1)} %get-tuple-element.23.own_ref), channel_id=1, source_target_pairs={{4,8},{12,16},{20,24},{28,32},{36,40},{44,48},{52,56},{60,64},{68,... | collective-permute-start | bytes 98312 | tf_op jit(solution)/shard_map/ppermute | solution.py:43
  56.5 1.9 %collective-permute-start.1 = (f32[64,128]{1,0:T(8,128)S(1)}, f32[64,128]{1,0:T(8,128)S(1)}, u32[]{:S(2)}, u32[]{:S(2)}) collective-permute-start(f32[64,128]{1,0:T(8,128)S(1)} %get-tuple-element.23.own_ref), channel_id=1, source_target_pairs={{0,4},{8,12},{16,20},{24,28},{32,36},{40,44},{48,52},{56,60},{64,6... | collective-permute-start | bytes 98312 | tf_op jit(solution)/shard_map/ppermute | solution.py:43
  58.4 0.5 shard_map.128.inner_ref
  58.9 4.7 %collective-permute-done.2 = f32[64,128]{1,0:T(8,128)S(1)} collective-permute-done((f32[64,128]{1,0:T(8,128)S(1)}, f32[64,128]{1,0:T(8,128)S(1)}, u32[]{:S(2)}, u32[]{:S(2)}) %collective-permute-start.2) | collective-permute-done | bytes 32800 | tf_op jit(solution)/shard_map/ppermute | solution.py:43
  63.7 0.0 collective-permute-done.1
  63.7 1.3 %shard_map.129 = (f32[8,64,128]{2,1,0:T(8,128)}, f32[64,128]{1,0:T(8,128)}) custom-call(f32[9,64,128]{2,1,0:T(8,128)S(1)} %shard_map.128.inner_ref, f32[64,128]{1,0:T(8,128)S(1)} %get-tuple-element.23.own_ref, f32[64,128]{1,0:T(8,128)S(1)} %get-tuple-element.29.west_ref, f32[64,128]{1,0:T(8,128)S(1)} %get-tuple-element.28.east_ref, f32[64,128]{1,0:T(8,128)S(1)} %copy-done.6, ...), custom_call_target="tpu_custom_call" | custom-call | flops 10000000 | bytes 2000000 | tf_op jit(solution)/shard_map/pallas_call | solution.py:23
  (11 shorter events, 0.0 us)
Async XLA Ops:
  2.9 5.0 %copy-start.6 = (f32[64,128]{1,0:T(8,128)S(1)}, f32[64,128]{1,0:T(8,128)}, u32[]{:S(2)}) copy-start(f32[64,128]{1,0:T(8,128)} %get-tuple-element.18.refs_2_.controls_ref) | copy-start | bytes 98308
  2.9 21.0 %all-to-all-start = ((bf16[4,288,128]{2,1,0:T(8,128)(2,1)}), bf16[4,288,128]{2,1,0:T(8,128)(2,1)S(1)}, u32[]{:S(2)}, u32[]{:S(2)}) async-start(bf16[4,288,128]{2,1,0:T(8,128)(2,1)} %get-tuple-element.15), calls=%async_computation | async-start | bytes 589824 | tf_op jit(solution)/shard_map/all_to_all | solution.py:422
  7.9 23.1 %collective-permute-start = (f32[64,128]{1,0:T(8,128)S(1)}, f32[64,128]{1,0:T(8,128)S(1)}, u32[]{:S(2)}, u32[]{:S(2)}) collective-permute-start(f32[64,128]{1,0:T(8,128)S(1)} %copy-done.6), channel_id=1, source_target_pairs={{12,16},{28,32},{44,48},{60,64},{76,80},{92,96},{108,112},{124,128... | collective-permute-start | bytes 98312 | tf_op jit(solution)/shard_map/ppermute | solution.py:57
  23.9 6.4 %copy-start = (bf16[8,4,2,32,128]{4,3,2,1,0:T(8,128)(2,1)S(1)}, bf16[8,4,2,32,128]{4,3,2,1,0:T(8,128)(2,1)}, u32[]{:S(2)}) copy-start(bf16[8,4,2,32,128]{4,3,2,1,0:T(8,128)(2,1)} %param.16) | copy-start | bytes 1572868
  24.6 5.7 %copy-start.1 = (f32[8,2,32,128]{3,2,1,0:T(8,128)S(1)}, f32[8,2,32,128]{3,2,1,0:T(8,128)}, u32[]{:S(2)}) copy-start(f32[8,2,32,128]{3,2,1,0:T(8,128)} %param.11) | copy-start | bytes 786436
  24.6 5.7 %copy-start.2 = (f32[2,32,128]{2,1,0:T(8,128)S(1)}, f32[2,32,128]{2,1,0:T(8,128)}, u32[]{:S(2)}) copy-start(f32[2,32,128]{2,1,0:T(8,128)} %param.13) | copy-start | bytes 98308
  24.6 5.7 %copy-start.3 = (f32[2,32,128]{2,1,0:T(8,128)S(1)}, f32[2,32,128]{2,1,0:T(8,128)}, u32[]{:S(2)}) copy-start(f32[2,32,128]{2,1,0:T(8,128)} %param.12) | copy-start | bytes 98308
  24.6 5.7 %copy-start.4 = (f32[2,32,128]{2,1,0:T(8,128)S(1)}, f32[2,32,128]{2,1,0:T(8,128)}, u32[]{:S(2)}) copy-start(f32[2,32,128]{2,1,0:T(8,128)} %param.14) | copy-start | bytes 98308
  24.6 5.7 %copy-start.5 = (f32[2,32,128]{2,1,0:T(8,128)S(1)}, f32[2,32,128]{2,1,0:T(8,128)}, u32[]{:S(2)}) copy-start(f32[2,32,128]{2,1,0:T(8,128)} %param.15) | copy-start | bytes 98308
  24.7 17.3 %all-to-all-start.1 = ((bf16[32,24,128]{2,1,0:T(8,128)(2,1)}), bf16[32,24,128]{2,1,0:T(8,128)(2,1)S(1)}, u32[]{:S(2)}, u32[]{:S(2)}) async-start(bf16[32,24,128]{2,1,0:T(8,128)(2,1)} %get-tuple-element.16), calls=%async_computation.1 | async-start | bytes 393216 | tf_op jit(solution)/shard_map/all_to_all | solution.py:435
  52.3 11.3 %collective-permute-start.2 = (f32[64,128]{1,0:T(8,128)S(1)}, f32[64,128]{1,0:T(8,128)S(1)}, u32[]{:S(2)}, u32[]{:S(2)}) collective-permute-start(f32[64,128]{1,0:T(8,128)S(1)} %get-tuple-element.23.own_ref), channel_id=1, source_target_pairs={{4,8},{12,16},{20,24},{28,32},{36,40},{44,48},{52,56},{60,64},{68,... | collective-permute-start | bytes 98312 | tf_op jit(solution)/shard_map/ppermute | solution.py:43
  56.5 7.2 %collective-permute-start.1 = (f32[64,128]{1,0:T(8,128)S(1)}, f32[64,128]{1,0:T(8,128)S(1)}, u32[]{:S(2)}, u32[]{:S(2)}) collective-permute-start(f32[64,128]{1,0:T(8,128)S(1)} %get-tuple-element.23.own_ref), channel_id=1, source_target_pairs={{0,4},{8,12},{16,20},{24,28},{32,36},{40,44},{48,52},{56,60},{64,6... | collective-permute-start | bytes 98312 | tf_op jit(solution)/shard_map/ppermute | solution.py:43

commit v6 on v5

--- a/solution.py
+++ b/solution.py
@@ -223,19 +223,16 @@
     x = x_ref[0]
     for at, ref in ((x - 1, west_ref), (x + 1, east_ref)):
         at = jnp.clip(at, 0, inner - 1)
-        edges = in_ref[at, high : high + rows, :].astype(F32)
-        ref[...] = edges + in_ref[at, high + rows : high + 2 * rows, :].astype(F32)
+        ref[...] = in_ref[at, high : high + rows, :].astype(F32)
 
 
 def first_body(fp_ref, counts_ref, rows_ref, values_ref, precision_ref, ens_ref, static_ref, e_ref, n_ref, out_ref, own_ref, full_ref):
     edges_body(ens_ref, static_ref, e_ref, n_ref, own_ref)
     message_body(fp_ref, counts_ref, rows_ref, values_ref, precision_ref, out_ref, full_ref)
     rows = own_ref.shape[0]
-    at = out_ref.shape[1] - 2 * rows
-    for piece in split_two(own_ref[...]):
-        for i in range(out_ref.shape[0]):
-            out_ref[i, at : at + rows, :] = piece
-        at += rows
+    at = out_ref.shape[1] - rows
+    for i in range(out_ref.shape[0]):
+        out_ref[i, at : at + rows, :] = own_ref[...].astype(BF16)
 
 
 def inner_increment_body(latitudes, scale, share, ens_ref, static_ref, sigma_ref, e_ref, n_ref, pert_ref, out_ref):
@@ -358,7 +355,7 @@
     members, _, columns = ens_out.shape
     lane = lanes_of(own_ref.shape)
     edge = at_edge(lane, columns)
-    packed = with_neighbours(own_ref[...], west_ref[...], east_ref[...], members + 1, lane)
+    packed = with_neighbours(own_ref[...], west_ref[...].astype(F32), east_ref[...].astype(F32), members + 1, lane)
     packed = smooth(packed, e_ref[...], n_ref[...]) + controls_ref[...]
     for f in range(members + 1):
         u = jnp.where(edge, place_edges(packed, f, lane), inner_ref[f])
@@ -403,7 +400,7 @@
     outer = len(runs)
     message, own = call(
         first_body,
-        (shape((RUN, room * outer + 2 * rows, columns), BF16), field),
+        (shape((RUN, room * outer + rows, columns), BF16), field),
         1e6,
         1e6,
         footprints[0, 0],
@@ -485,7 +482,7 @@
         pert,
         sigma,
     )
-    west, east = from_neighbours(own_source, "tile")
+    west, east = from_neighbours(own_source.astype(BF16), "tile")
     inner = call(
         lambda *refs: inner_result_body(latitudes, *refs),
         shape(source.shape),

time: 65.4 us -> 64.4 us (0.985)
  transfers between devices with their start and end apart: 5 -> 5, of which waited for: 2 -> 1; matrix products, arithmetic and copies ran while one was open for 0% -> 0% of each run, Pallas kernels for 4% -> 4%
where the time goes in v6:
time: 64.4 us; the launch traced here: 64 us
  starting transfers between devices  32.3 us (50%)
  blocking collectives  19 us (30%)
  Pallas kernels  7.61 us (12%)
  waiting for transfers between devices  4.25 us (7%)
  between operations  0.82 us (1%)
    ppermute x1, starting transfers between devices, between_runs(): return lax.ppermute(x, axis, pairs + [(j, i) for i, j in pairs])  15.9 us
    all_gather x1, blocking collectives, on_device(): parts = lax.all_gather(partial, 'mem')  9.94 us
    all_gather x1, blocking collectives, on_device(): grad_parts = lax.all_gather(partial_grad, 'mem')  9.02 us
    pallas_call x8, Pallas kernels, call(): pl.pallas_call(body, out_shape=out, in_specs=specs or [spec] * len(operan...  7.61 us
    ppermute x2, starting transfers between devices, from_neighbours(): swaps.append(lax.ppermute(x, axis, pairs + [(j, i) for i, j in pairs]))  6.18 us
    all_to_all x1, starting transfers between devices, on_device(): lax.all_to_all(message, 'tile', 0, 0, axis_index_groups=across, tiled=True)  5.18 us
    all_to_all x1, starting transfers between devices, on_device(): lax.all_to_all(message, 'tile', 0, 0, axis_index_groups=runs, tiled=True)  4.97 us
    ppermute x2, waiting for transfers between devices, from_neighbours(): swaps.append(lax.ppermute(x, axis, pairs + [(j, i) for i, j in pairs]))  4.21 us
  transfers between devices with their start and end apart: 5, of which 1 were waited for; matrix products, arithmetic and copies ran while one was open for 0% of the time, Pallas kernels for 4%

profile of v6, /device:TPU:1, one launch (start us, length us, event | category | flops | bytes accessed | tf_op | source)
XLA Modules:
  0.0 64.0 jit_solution(1444990825007909352)
XLA Ops:
  0.6 2.2 %shard_map.122 = (bf16[4,224,128]{2,1,0:T(8,128)(2,1)}, f32[64,128]{1,0:T(8,128)}) custom-call(bf16[128,4,128]{2,1,0:T(4,128)(2,1)} %bitcast.46, s32[1,128]{1,0:T(1,128)} %bitcast.50, s32[4,128]{1,0:T(4,128)} %bitcast.47, f32[4,128]{1,0:T(4,128)} %bitcast.48, f32[4,128]{1,0:T(4,128)} %bitcast.49, f32[8,64,128]{2,1,0:T(8,128)} %bitcast.28, ...), custom_call_target="tpu_custom_call" | custom-call | flops 1000000 | bytes 1000000 | tf_op jit(solution)/shard_map/pallas_call | solution.py:23
  2.9 5.0 %all-to-all-start = ((bf16[4,224,128]{2,1,0:T(8,128)(2,1)}), bf16[4,224,128]{2,1,0:T(8,128)(2,1)S(1)}, u32[]{:S(2)}, u32[]{:S(2)}) async-start(bf16[4,224,128]{2,1,0:T(8,128)(2,1)} %get-tuple-element.15), calls=%async_computation | async-start | bytes 458752 | tf_op jit(solution)/shard_map/all_to_all | solution.py:419
  7.8 0.0 copy-done.2
  7.9 15.9 %collective-permute-start = (f32[64,128]{1,0:T(8,128)S(1)}, f32[64,128]{1,0:T(8,128)S(1)}, u32[]{:S(2)}, u32[]{:S(2)}) collective-permute-start(f32[64,128]{1,0:T(8,128)S(1)} %copy-done.2), channel_id=1, source_target_pairs={{12,16},{28,32},{44,48},{60,64},{76,80},{92,96},{108,112},{124,128... | collective-permute-start | bytes 98312 | tf_op jit(solution)/shard_map/ppermute | solution.py:57
  23.8 0.0 all-to-all-done.in_ref
  23.8 0.0 copy-start
  23.8 0.8 %shard_map.123 = (bf16[32,24,128]{2,1,0:T(8,128)(2,1)}, f32[64,128]{1,0:T(8,128)S(1)}, f32[64,128]{1,0:T(8,128)S(1)}) custom-call(s32[1]{0:T(128)} %bitcast.x_ref.refs_0_, bf16[4,224,128]{2,1,0:T(8,128)(2,1)S(1)} %all-to-all-done.in_ref), custom_call_target="tpu_custom_call" | custom-call | flops 20000000000 | bytes 1000000 | tf_op jit(solution)/shard_map/pallas_call | solution.py:23
  24.6 0.0 copy-start.6
  24.6 5.2 %all-to-all-start.1 = ((bf16[32,24,128]{2,1,0:T(8,128)(2,1)}), bf16[32,24,128]{2,1,0:T(8,128)(2,1)S(1)}, u32[]{:S(2)}, u32[]{:S(2)}) async-start(bf16[32,24,128]{2,1,0:T(8,128)(2,1)} %get-tuple-element.16), calls=%async_computation.1 | async-start | bytes 393216 | tf_op jit(solution)/shard_map/all_to_all | solution.py:432
  29.8 0.0 copy-done
  29.9 0.6 shard_map.124.refs_1_
  30.5 0.0 collective-permute-done.refs_3_
  30.5 0.9 %shard_map.125 = (s16[272,128]{1,0:T(8,128)(2,1)S(1)}, f32[64,128]{1,0:T(8,128)S(1)}, f32[64,128]{1,0:T(8,128)S(1)}) custom-call(s32[1]{0:T(128)} %bitcast.x_ref.refs_0_, f32[256,128]{1,0:T(8,128)S(1)} %shard_map.124.refs_1_, f32[64,128]{1,0:T(8,128)S(1)} %copy-done.2, f32[64,128]{1,0:T(8,128)S(1)} %collective-permute-done.refs_3_, ...), custom_call_target="tpu_custom_call" | custom-call | flops 4000000000 | bytes 4000000 | tf_op jit(solution)/shard_map/pallas_call | solution.py:23
  31.4 9.9 %all-gather = s16[1088,128]{1,0:T(8,128)(2,1)S(1)} all-gather(s16[272,128]{1,0:T(8,128)(2,1)S(1)} %get-tuple-element.21), channel_id=2, replica_groups=mesh['tile'=128,'mem'=4] {'mem'}, dimensions={0}, use_global_device_ids=true | all-gather | bytes 348160 | tf_op jit(solution)/shard_map/all_gather | solution.py:466
  41.4 0.0 all-to-all-done.1
  41.4 1.0 %shard_map.126 = s16[272,128]{1,0:T(8,128)(2,1)S(1)} custom-call(s16[4,272,128]{2,1,0:T(8,128)(2,1)S(1)} %bitcast.27, bf16[768,128]{1,0:T(8,128)(2,1)S(1)} %bitcast.31), custom_call_target="tpu_custom_call" | custom-call | flops 300000000 | bytes 4000000 | tf_op jit(solution)/shard_map/pallas_call | solution.py:23
  42.4 9.0 %all-gather.1 = s16[1088,128]{1,0:T(8,128)(2,1)S(1)} all-gather(s16[272,128]{1,0:T(8,128)(2,1)S(1)} %shard_map.126), channel_id=3, replica_groups=mesh['tile'=128,'mem'=4] {'mem'}, dimensions={0}, use_global_device_ids=true | all-gather | bytes 348160 | tf_op jit(solution)/shard_map/all_gather | solution.py:475
  51.4 0.3 shard_map.127
  51.7 4.3 %collective-permute-start.2 = (bf16[64,128]{1,0:T(8,128)(2,1)S(1)}, bf16[64,128]{1,0:T(8,128)(2,1)S(1)}, u32[]{:S(2)}, u32[]{:S(2)}) collective-permute-start(bf16[64,128]{1,0:T(8,128)(2,1)S(1)} %convert_element_type.3), channel_id=1, source_target_pairs={{4,8},{12,16},{20,24},{28,32},{36,40},{44,48},{52,56},{60,64},{68,... | collective-permute-start | bytes 49160 | tf_op jit(solution)/shard_map/ppermute | solution.py:43
  56.0 1.9 %collective-permute-start.1 = (bf16[64,128]{1,0:T(8,128)(2,1)S(1)}, bf16[64,128]{1,0:T(8,128)(2,1)S(1)}, u32[]{:S(2)}, u32[]{:S(2)}) collective-permute-start(bf16[64,128]{1,0:T(8,128)(2,1)S(1)} %convert_element_type.3), channel_id=1, source_target_pairs={{0,4},{8,12},{16,20},{24,28},{32,36},{40,44},{48,52},{56,60},{64,6... | collective-permute-start | bytes 49160 | tf_op jit(solution)/shard_map/ppermute | solution.py:43
  57.9 0.5 shard_map.128.inner_ref
  58.5 4.2 %collective-permute-done.2 = bf16[64,128]{1,0:T(8,128)(2,1)S(1)} collective-permute-done((bf16[64,128]{1,0:T(8,128)(2,1)S(1)}, bf16[64,128]{1,0:T(8,128)(2,1)S(1)}, u32[]{:S(2)}, u32[]{:S(2)}) %collective-permute-start.2) | collective-permute-done | bytes 16416 | tf_op jit(solution)/shard_map/ppermute | solution.py:43
  62.7 0.0 collective-permute-done.1
  62.7 1.3 %shard_map.129 = (f32[8,64,128]{2,1,0:T(8,128)}, f32[64,128]{1,0:T(8,128)}) custom-call(f32[9,64,128]{2,1,0:T(8,128)S(1)} %shard_map.128.inner_ref, f32[64,128]{1,0:T(8,128)S(1)} %get-tuple-element.23.own_ref, bf16[64,128]{1,0:T(8,128)(2,1)S(1)} %get-tuple-element.29.west_ref, bf16[64,128]{1,0:T(8,128)(2,1)S(1)} %get-tuple-element.28.east_ref, ...), custom_call_target="tpu_custom_call" | custom-call | flops 10000000 | bytes 2000000 | tf_op jit(solution)/shard_map/pallas_call | solution.py:23
  (12 shorter events, 0.0 us)
Async XLA Ops:
  2.9 5.0 %copy-start.2 = (f32[64,128]{1,0:T(8,128)S(1)}, f32[64,128]{1,0:T(8,128)}, u32[]{:S(2)}) copy-start(f32[64,128]{1,0:T(8,128)} %get-tuple-element.18.refs_2_.controls_ref) | copy-start | bytes 98308
  2.9 21.0 %all-to-all-start = ((bf16[4,224,128]{2,1,0:T(8,128)(2,1)}), bf16[4,224,128]{2,1,0:T(8,128)(2,1)S(1)}, u32[]{:S(2)}, u32[]{:S(2)}) async-start(bf16[4,224,128]{2,1,0:T(8,128)(2,1)} %get-tuple-element.15), calls=%async_computation | async-start | bytes 458752 | tf_op jit(solution)/shard_map/all_to_all | solution.py:419
  7.9 22.6 %collective-permute-start = (f32[64,128]{1,0:T(8,128)S(1)}, f32[64,128]{1,0:T(8,128)S(1)}, u32[]{:S(2)}, u32[]{:S(2)}) collective-permute-start(f32[64,128]{1,0:T(8,128)S(1)} %copy-done.2), channel_id=1, source_target_pairs={{12,16},{28,32},{44,48},{60,64},{76,80},{92,96},{108,112},{124,128... | collective-permute-start | bytes 98312 | tf_op jit(solution)/shard_map/ppermute | solution.py:57
  23.8 6.0 %copy-start = (bf16[8,4,2,32,128]{4,3,2,1,0:T(8,128)(2,1)S(1)}, bf16[8,4,2,32,128]{4,3,2,1,0:T(8,128)(2,1)}, u32[]{:S(2)}) copy-start(bf16[8,4,2,32,128]{4,3,2,1,0:T(8,128)(2,1)} %param.16) | copy-start | bytes 1572868
  24.6 5.2 %copy-start.1 = (f32[8,2,32,128]{3,2,1,0:T(8,128)S(1)}, f32[8,2,32,128]{3,2,1,0:T(8,128)}, u32[]{:S(2)}) copy-start(f32[8,2,32,128]{3,2,1,0:T(8,128)} %param.11) | copy-start | bytes 786436
  24.6 5.2 %copy-start.3 = (f32[2,32,128]{2,1,0:T(8,128)S(1)}, f32[2,32,128]{2,1,0:T(8,128)}, u32[]{:S(2)}) copy-start(f32[2,32,128]{2,1,0:T(8,128)} %param.13) | copy-start | bytes 98308
  24.6 5.2 %copy-start.4 = (f32[2,32,128]{2,1,0:T(8,128)S(1)}, f32[2,32,128]{2,1,0:T(8,128)}, u32[]{:S(2)}) copy-start(f32[2,32,128]{2,1,0:T(8,128)} %param.12) | copy-start | bytes 98308
  24.6 5.2 %copy-start.5 = (f32[2,32,128]{2,1,0:T(8,128)S(1)}, f32[2,32,128]{2,1,0:T(8,128)}, u32[]{:S(2)}) copy-start(f32[2,32,128]{2,1,0:T(8,128)} %param.14) | copy-start | bytes 98308
  24.6 5.3 %copy-start.6 = (f32[2,32,128]{2,1,0:T(8,128)S(1)}, f32[2,32,128]{2,1,0:T(8,128)}, u32[]{:S(2)}) copy-start(f32[2,32,128]{2,1,0:T(8,128)} %param.15) | copy-start | bytes 98308
  24.6 16.8 %all-to-all-start.1 = ((bf16[32,24,128]{2,1,0:T(8,128)(2,1)}), bf16[32,24,128]{2,1,0:T(8,128)(2,1)S(1)}, u32[]{:S(2)}, u32[]{:S(2)}) async-start(bf16[32,24,128]{2,1,0:T(8,128)(2,1)} %get-tuple-element.16), calls=%async_computation.1 | async-start | bytes 393216 | tf_op jit(solution)/shard_map/all_to_all | solution.py:432
  51.7 11.0 %collective-permute-start.2 = (bf16[64,128]{1,0:T(8,128)(2,1)S(1)}, bf16[64,128]{1,0:T(8,128)(2,1)S(1)}, u32[]{:S(2)}, u32[]{:S(2)}) collective-permute-start(bf16[64,128]{1,0:T(8,128)(2,1)S(1)} %convert_element_type.3), channel_id=1, source_target_pairs={{4,8},{12,16},{20,24},{28,32},{36,40},{44,48},{52,56},{60,64},{68,... | collective-permute-start | bytes 49160 | tf_op jit(solution)/shard_map/ppermute | solution.py:43
  56.0 6.7 %collective-permute-start.1 = (bf16[64,128]{1,0:T(8,128)(2,1)S(1)}, bf16[64,128]{1,0:T(8,128)(2,1)S(1)}, u32[]{:S(2)}, u32[]{:S(2)}) collective-permute-start(bf16[64,128]{1,0:T(8,128)(2,1)S(1)} %convert_element_type.3), channel_id=1, source_target_pairs={{0,4},{8,12},{16,20},{24,28},{32,36},{40,44},{48,52},{56,60},{64,6... | collective-permute-start | bytes 49160 | tf_op jit(solution)/shard_map/ppermute | solution.py:43
